TPU v7x, 512 devices: a whole 4x8x8 slice. The times are simulated.
512 devices in a mesh: dp: 64 (over y, z), graph: 8 (over x, core).
Axes of the slice: x: 4, y: 8, z: 8, core: 2. Of those that a mesh axis runs over, the one named last changes fastest.
Arguments:
- atoms: bfloat16 [64, 192, 512], P('dp', 'graph'), may hold values from -6 to 6
- cotangent: bfloat16 [64, 192, 512], P('dp', 'graph'), may hold values from -6 to 6
- sources: int32 [64, 4096], P('dp', 'graph'), may hold values from 0 to 191
- targets: int32 [64, 4096], P('dp', 'graph'), may hold values from 0 to 191
- radial: bfloat16 [64, 4096, 128], P('dp', 'graph'), may hold values from 0 to 1
- envelope: float32 [64, 4096], P('dp', 'graph'), may hold values from 0.1 to 1
- edge_counts: int32 [64, 8], P('dp', 'graph'), may hold values from 128 to 512
- source_weight: bfloat16 [512, 1024], replicated, may hold values from -0.25 to 0.25
- radial_weight: bfloat16 [128, 1024], replicated, may hold values from -0.5 to 0.5
- output_weight: bfloat16 [1024, 512], replicated, may hold values from -0.1875 to 0.1875
Outputs:
- updated: bfloat16 [64, 192, 512], P('dp', 'graph')
- grad_atoms: bfloat16 [64, 192, 512], P('dp', 'graph')
- grad_source: bfloat16 [512, 1024], replicated
- grad_output: bfloat16 [1024, 512], replicated
All inputs are finite; a program needn't handle non-finite values.
Results may differ from a plain program's by a relative error of at most 0.0057.
Values may be sent and summed in bfloat16 or wider, within the bound.
A program may use at most 64 MiB of HBM per device.

v0:
```python
import math

import jax
import jax.numpy as jnp
from jax import lax
from jax.sharding import PartitionSpec as P


def contract_rows(left, right):
    return lax.dot_general(
        left, right, (((0,), (0,)), ((), ())), preferred_element_type=jnp.float32
    )


def contract_cols(left, right):
    return lax.dot_general(
        left, right, (((1,), (1,)), ((), ())), preferred_element_type=jnp.float32
    )


def local(
    atoms,
    cotangent,
    sources,
    targets,
    radial,
    envelope,
    edge_counts,
    source_weight,
    radial_weight,
    output_weight,
):
    embed = atoms[0]
    adjoint = cotangent[0]
    src_ids = sources[0]
    dst_ids = targets[0]
    basis = radial[0]
    decay = envelope[0]
    count = edge_counts[0, 0]
    own_atoms = embed.shape[0]
    slot_count = src_ids.shape[0]
    scale = math.sqrt(own_atoms / slot_count)
    total_atoms = own_atoms * lax.axis_size("graph")
    embed_full = lax.all_gather(embed, "graph", axis=0, tiled=True)
    columns = jnp.arange(total_atoms, dtype=jnp.int32)[None, :]
    onehot_src = (src_ids[:, None] == columns).astype(jnp.bfloat16)
    onehot_dst = (dst_ids[:, None] == columns).astype(jnp.bfloat16)
    gathered = jnp.dot(onehot_src, embed_full, preferred_element_type=jnp.float32).astype(
        jnp.bfloat16
    )
    pre = jnp.dot(basis, radial_weight, preferred_element_type=jnp.float32) + jnp.dot(
        gathered, source_weight, preferred_element_type=jnp.float32
    )
    live = (jnp.arange(slot_count, dtype=jnp.int32) < count).astype(jnp.float32)
    weight = decay * live
    sigma = jax.nn.sigmoid(pre)
    message = (pre * sigma * weight[:, None]).astype(jnp.bfloat16)
    partial_sum = contract_rows(onehot_dst, message)
    summed = lax.psum_scatter(partial_sum, "graph", scatter_dimension=0, tiled=True).astype(
        jnp.bfloat16
    )
    update = jnp.dot(summed, output_weight, preferred_element_type=jnp.float32) * scale
    updated = (embed.astype(jnp.float32) + update).astype(jnp.bfloat16)
    out_term = contract_rows(summed, adjoint) * scale
    back_own = (contract_cols(adjoint, output_weight) * scale).astype(jnp.bfloat16)
    back_full = lax.all_gather(back_own, "graph", axis=0, tiled=True)
    pulled = jnp.dot(onehot_dst, back_full, preferred_element_type=jnp.float32)
    slope = sigma * (1.0 + pre * (1.0 - sigma))
    dpre = (pulled * weight[:, None] * slope).astype(jnp.bfloat16)
    source_term = contract_rows(gathered, dpre)
    dgathered = contract_cols(dpre, source_weight).astype(jnp.bfloat16)
    pushed_part = contract_rows(onehot_src, dgathered)
    pushed = lax.psum_scatter(pushed_part, "graph", scatter_dimension=0, tiled=True)
    grad_atoms = (adjoint.astype(jnp.float32) + pushed).astype(jnp.bfloat16)
    systems_all = lax.axis_size("dp")
    source_factor = 16.0 / math.sqrt(systems_all * slot_count * lax.axis_size("graph"))
    source_total, out_total = lax.psum((source_term, out_term), ("dp", "graph"))
    grad_source = (source_total * source_factor).astype(jnp.bfloat16)
    grad_output = (out_total * (1.0 / math.sqrt(systems_all * total_atoms))).astype(jnp.bfloat16)
    return (updated[None], grad_atoms[None], grad_source, grad_output)


def solution(mesh):
    in_specs = (
        P("dp", "graph", None),
        P("dp", "graph", None),
        P("dp", "graph"),
        P("dp", "graph"),
        P("dp", "graph", None),
        P("dp", "graph"),
        P("dp", "graph"),
        P(),
        P(),
        P(),
    )
    out_specs = (P("dp", "graph", None), P("dp", "graph", None), P(), P())
    return jax.shard_map(local, mesh=mesh, in_specs=in_specs, out_specs=out_specs, check_vma=False)
```

profile of v0, /device:TPU:1, one launch (start us, length us, event | category | flops | bytes accessed | tf_op | source)
XLA Modules:
  0.0 408.7 jit_solution(14051451329866867120)
XLA Ops:
  7.2 0.0 reduce-scatter.3.cloned.1.call-start
  8.0 19.7 %all-gather = bf16[1,192,512]{2,1,0:T(8,128)(2,1)S(1)} all-gather(bf16[1,24,512]{2,1,0:T(8,128)(2,1)} %param.10), channel_id=2, replica_groups=mesh['dp'=64,'graph'=8] {'graph'}, dimensions={1}, use_global_device_ids=true | all-gather | bytes 221184 | tf_op jit(solution)/shard_map/all_gather | solution.py:44
  27.7 0.7 fusion.18
  28.4 1.0 convolution_convert_fusion.1
  29.4 1.4 fusion.11
  30.9 0.7 convolution_add_fusion
  31.6 1.3 copy-done.3
  32.9 1.8 fusion.5
  34.7 0.0 reduce-scatter.3.cloned.1.call-update
  34.7 0.0 reduce-scatter.5.cloned.1.call-start
  34.8 0.4 fusion.1
  35.2 13.0 %all_gather.7 = bf16[192,1024]{1,0:T(8,128)(2,1)S(1)} all-gather(bf16[24,1024]{1,0:T(8,128)(2,1)S(1)} %fusion.1), channel_id=1, replica_groups=mesh['dp'=64,'graph'=8] {'graph'}, dimensions={0}, use_global_device_ids=true | all-gather | bytes 442368 | tf_op jit(solution)/shard_map/all_gather | solution.py:66
  48.1 3.5 multiply_convert_fusion.2
  51.7 2.9 fusion
  54.6 0.0 all-reduce.3.cloned.1.call-start
  54.7 3.3 fusion.20
  58.0 10.5 %reduce-scatter.3.cloned.1.call-done = f32[24,1024]{1,0:T(8,128)} async-done(((f32[192,1024]{1,0:T(8,128)}), f32[24,1024]{1,0:T(8,128)}) %reduce-scatter.3.cloned.1.call-update) | async-done | bytes 98320 | tf_op jit(solution)/shard_map/reduce_scatter | solution.py:59
  68.4 2.7 convolution_multiply_fusion
  71.2 35.4 %reduce-scatter.5.cloned.1.call-done = f32[24,512]{1,0:T(8,128)} async-done(((f32[192,512]{1,0:T(8,128)}), f32[24,512]{1,0:T(8,128)}) %reduce-scatter.5.cloned.1.call-update) | async-done | bytes 49168 | tf_op jit(solution)/shard_map/reduce_scatter | solution.py:73
  106.5 1.4 fusion.13
  108.0 0.9 fusion.4
  108.8 289.2 %all-reduce.3.cloned.1.call-done = (f32[512,1024]{1,0:T(8,128)}, f32[1024,512]{1,0:T(8,128)}) async-done(((f32[512,1024]{1,0:T(8,128)}, f32[1024,512]{1,0:T(8,128)}), (f32[512,1024]{1,0:T(8,128)}, f32[1024,512]{1,0:T(8,128)})) %all-reduce.3.cloned.1.call-update) | async-done | bytes 4194320 | tf_op jit(solution)/shard_map/psum | solution.py:77
  398.0 3.0 multiply_convert_fusion.1
  401.0 1.3 multiply_convert_fusion
  (19 shorter events, 0.1 us)
Async XLA Ops:
  7.2 23.7 %copy-start = (bf16[512,1024]{1,0:T(8,128)(2,1)S(1)}, bf16[512,1024]{1,0:T(8,128)(2,1)}, u32[]{:S(2)}) copy-start(bf16[512,1024]{1,0:T(8,128)(2,1)} %param.17) | copy-start | bytes 3145732
  7.2 61.3 %reduce-scatter.3.cloned.1.call-start = ((), (), s32[]{:S(2)}) async-start(), calls=%async_computation.2 | async-start | bytes 884736 | tf_op jit(solution)/shard_map/reduce_scatter | solution.py:59
  30.8 2.1 copy-start.8
  31.6 1.3 copy-start.3
  32.9 1.8 copy-start.1
  32.9 1.8 copy-start.5
  34.7 71.8 %reduce-scatter.5.cloned.1.call-start = ((), (), s32[]{:S(2)}) async-start(), calls=%async_computation.3 | async-start | bytes 442368 | tf_op jit(solution)/shard_map/reduce_scatter | solution.py:73
  48.1 3.5 copy-start.7
  54.6 343.4 %all-reduce.3.cloned.1.call-start = ((), (), s32[]{:S(2)}) async-start(), calls=%async_computation.4 | async-start | bytes 8388608 | tf_op jit(solution)/shard_map/psum | solution.py:77
  71.1 36.8 %copy-start.4 = (f32[24,1024]{1,0:T(8,128)S(1)}, f32[24,1024]{1,0:T(8,128)}, u32[]{:S(2)}) copy-start(f32[24,1024]{1,0:T(8,128)} %reduce-scatter.3.cloned.1.call-done) | copy-start | bytes 294916
  71.1 36.8 %copy-start.6 = (bf16[1,24,512]{2,1,0:T(8,128)(2,1)S(1)}, bf16[1,24,512]{2,1,0:T(8,128)(2,1)}, u32[]{:S(2)}) copy-start(bf16[1,24,512]{2,1,0:T(8,128)(2,1)} %param.10) | copy-start | bytes 73732
  398.0 3.0 copy-start.2
Sparse Core Ops, SparseCore 0:
  34.8 33.5 reduce-scatter.2
  71.5 35.0 reduce-scatter.4
  111.7 286.2 all-reduce.2
where the time goes:
time: 410 us; the launch traced here: 409 us
  waiting for transfers between devices  335 us (82%)
  blocking collectives  32.7 us (8%)
  matrix products  18.6 us (5%)
  between operations  14.5 us (4%)
  other arithmetic  6.33 us (2%)
    psum x1, waiting for transfers between devices, local(): source_total, out_total = lax.psum((source_term, out_term), ('dp', 'graph'))  289 us
    reduce_scatter x1, waiting for transfers between devices, local(): lax.psum_scatter(pushed_part, 'graph', scatter_dimension=0, tiled=True)  35.4 us
    all_gather x1, blocking collectives, local(): embed_full = lax.all_gather(embed, 'graph', axis=0, tiled=True)  19.7 us
    all_gather x1, blocking collectives, local(): back_full = lax.all_gather(back_own, 'graph', axis=0, tiled=True)  13 us
    dot_general x4, matrix products, contract_rows(): lax.dot_general(left, right, (((0,), (0,)), ((), ())), preferred_element_...  10.7 us
    reduce_scatter x1, waiting for transfers between devices, local(): lax.psum_scatter(partial_sum, 'graph', scatter_dimension=0, tiled=True)  10.5 us
  transfers between devices with their start and end apart: 3, of which 3 were waited for; matrix products, arithmetic and copies ran while one was open for 4% of the time, Pallas kernels for 0%

commit v1 on v0

v1 whole, which is shorter than its diff:
```python
import functools
import math

import jax
import jax.numpy as jnp
from jax import lax
from jax.experimental import pallas as pl
from jax.experimental.pallas import tpu as pltpu
from jax.sharding import PartitionSpec as P

MESH = pl.DeviceIdType.MESH
F32 = jnp.float32
BF16 = jnp.bfloat16

OWN = 24
SLOT = 2 * OWN
ATOMS = 192
EDGES = 512
DA = 512
DE = 1024
PAD = 32
COLS = 128
SIDE = 8


def dot(left, right):
    return jnp.dot(left, right, preferred_element_type=F32)


def dot_nt(left, right):
    return lax.dot_general(left, right, (((1,), (1,)), ((), ())), preferred_element_type=F32)


def dot_tn(left, right):
    return lax.dot_general(left, right, (((0,), (0,)), ((), ())), preferred_element_type=F32)


def body(
    atoms_ref,
    cot_ref,
    src_ref,
    dst_ref,
    radial_ref,
    env_ref,
    count_ref,
    sw_ref,
    rw_ref,
    ow_ref,
    updated_ref,
    grad_atoms_ref,
    out1,
    out2,
    full,
    atoms_s,
    back_s,
    gathered_s,
    hot_dst_s,
    hott_src_s,
    hott_dst_s,
    cols_s,
    msg_s,
    dpre_s,
    stage,
    recv,
    rows_out,
    rows_in,
    ga,
    gb,
    ra,
    rb,
    sa,
    sb,
    qa,
    qb,
    fa,
    fb,
    full_send,
    full_recv,
    rs_send,
    rs_recv,
    row_send,
    row_recv,
    r1_send,
    r1_recv,
    r2_send,
    r2_recv,
    r3_send,
    r3_recv,
    r4_send,
    r4_recv,
    x_send,
    x_recv,
    c_send,
    c_recv,
):
    dp = lax.axis_index("dp")
    g = lax.axis_index("graph")
    y, z = lax.div(dp, SIDE), lax.rem(dp, SIDE)
    x, core = lax.div(g, 2), lax.rem(g, 2)
    other = 1 - core
    scale = math.sqrt(OWN / EDGES)
    sends = []

    def copy(src, dst, send, recv_sem, device):
        c = pltpu.make_async_remote_copy(
            src_ref=src, dst_ref=dst, send_sem=send, recv_sem=recv_sem, device_id=device, device_id_type=MESH
        )
        c.start()
        sends.append(c)

    def arrived(dst, recv_sem):
        pltpu.make_async_remote_copy(
            src_ref=dst, dst_ref=dst, send_sem=recv_sem, recv_sem=recv_sem, device_id=(dp, g), device_id_type=MESH
        ).wait_recv()

    graph_peers = [(dp, lax.rem(g + k, 8)) for k in range(1, 8)]
    y_at = [lax.rem(y + k, SIDE) for k in range(SIDE)]
    z_at = [lax.rem(z + k, SIDE) for k in range(SIDE)]
    y_peers = [(y_at[k] * SIDE + z, g) for k in range(SIDE)]
    z_peers = [(y * SIDE + z_at[k], g) for k in range(SIDE)]

    barrier = pltpu.get_barrier_semaphore()
    for peer in graph_peers + y_peers[1:] + z_peers[1:]:
        pl.semaphore_signal(barrier, inc=1, device_id=peer, device_id_type=MESH)

    full[g] = jnp.concatenate([atoms_ref[0], cot_ref[0]], axis=0)
    pl.semaphore_wait(barrier, 21)
    for k in range(1, 8):
        copy(full.at[g], full.at[g], full_send.at[k], full_recv.at[g], graph_peers[k - 1])

    src_row = src_ref[...]
    dst_row = dst_ref[...]
    slots = lax.broadcasted_iota(jnp.int32, (1, EDGES), 1)
    live = (slots < count_ref[0, 0]).astype(F32)
    weight_row = env_ref[...] * live
    table = jnp.concatenate(
        [src_row.astype(F32), dst_row.astype(F32), weight_row, jnp.zeros((5, EDGES), F32)], axis=0
    )
    cols_s[...] = table.T
    atom_rows = lax.broadcasted_iota(jnp.int32, (ATOMS, EDGES), 0)
    hott_src_s[...] = (atom_rows == src_row).astype(F32).astype(BF16)
    hott_dst_s[...] = (atom_rows == dst_row).astype(F32).astype(BF16)
    atom_cols = lax.broadcasted_iota(jnp.int32, (EDGES, ATOMS), 1).astype(F32)
    hot_src = (atom_cols == cols_s[:, 0:1]).astype(F32).astype(BF16)
    hot_dst_s[...] = (atom_cols == cols_s[:, 1:2]).astype(F32).astype(BF16)
    pick_r = lax.broadcasted_iota(jnp.int32, (ATOMS, 8 * SLOT), 0)
    pick_c = lax.broadcasted_iota(jnp.int32, (ATOMS, 8 * SLOT), 1)
    pick_at = pick_r + OWN * ((pick_r * 683) >> 14)
    pick_atoms = (pick_c == pick_at).astype(F32).astype(BF16)
    pick_cot = (pick_c == pick_at + OWN).astype(F32).astype(BF16)

    for k in range(1, 8):
        peer = lax.rem(g + k, 8)
        arrived(full.at[peer], full_recv.at[peer])
    both = full[...].reshape(8 * SLOT, DA)
    atoms = dot(pick_atoms, both).astype(BF16)
    cot = dot(pick_cot, both).astype(BF16)
    atoms_s[0] = atoms
    atoms_s[1] = cot
    gathered_s[...] = dot(hot_src, atoms).astype(BF16)
    back_s[...] = (dot_nt(cot, ow_ref[...]) * scale).astype(BF16)

    for dx in (2, 1, 3, 0):
        xt = lax.rem(x + dx, 4)
        cols = pl.ds(pl.multiple_of(xt * 2 * COLS, 2 * COLS), 2 * COLS)
        for r in range(4):
            rows = slice(r * 128, (r + 1) * 128)
            pre = dot(radial_ref[0, rows, :], rw_ref[:, cols]) + dot(gathered_s[rows, :], sw_ref[:, cols])
            pulled = dot(hot_dst_s[rows, :], back_s[:, cols])
            weight = cols_s[rows, 2:3]
            sigma = jax.nn.sigmoid(pre)
            msg_s[rows, :] = (pre * sigma * weight).astype(BF16)
            slope = sigma * (1.0 + pre * (1.0 - sigma))
            dpre_s[rows, :] = (pulled * weight * slope).astype(BF16)
        part = dot(hott_dst_s[...], msg_s[...]).astype(BF16)
        stage[dx, 0, 0] = part[:, :COLS]
        stage[dx, 1, 0] = part[:, COLS:]
        part = dot(hott_src_s[...], dpre_s[...]).astype(BF16)
        stage[dx, 0, 1] = part[:, :COLS]
        stage[dx, 1, 1] = part[:, COLS:]
        if dx:
            for cc in range(2):
                copy(
                    stage.at[dx, cc],
                    recv.at[2 * dx + core],
                    rs_send.at[2 * dx + cc],
                    rs_recv.at[2 * dx + core],
                    (dp, 2 * xt + cc),
                )
        else:
            copy(stage.at[0, other], recv.at[core], rs_send.at[0], rs_recv.at[core], (dp, 2 * x + other))

    total = stage[0, core].astype(F32)
    for slot in (other, 4, 5, 2, 3, 6, 7):
        arrived(recv.at[slot], rs_recv.at[slot])
        total = total + recv[slot].astype(F32)
    sums = total.astype(BF16)
    summed, dsum = sums[0], sums[1]

    grow_r = lax.broadcasted_iota(jnp.int32, (8 * PAD, ATOMS), 0)
    grow_c = lax.broadcasted_iota(jnp.int32, (8 * PAD, ATOMS), 1)
    inner = grow_r & (PAD - 1)
    grow = ((inner < OWN) & (grow_c == (grow_r >> 5) * OWN + inner)).astype(F32).astype(BF16)
    rows_out[:, 0] = dot(grow, summed).astype(BF16).reshape(8, PAD, COLS)
    rows_out[:, 1] = dot(grow, dsum).astype(BF16).reshape(8, PAD, COLS)
    own_cols = pl.ds(pl.multiple_of(g * COLS, COLS), COLS)
    rows_in[:, :, own_cols] = rows_out[g]

    ga[...] = dot_tn(summed, atoms_s[1]).astype(BF16).reshape(SIDE, 16, DA)
    gb[...] = dot_tn(atoms_s[0], dsum).astype(BF16).reshape(SIDE, 64, COLS)
    for k in range(1, SIDE):
        copy(ga.at[y_at[k]], ra.at[k], r1_send.at[0, k], r1_recv.at[0, k], y_peers[k])
        copy(gb.at[z_at[k]], rb.at[k], r1_send.at[1, k], r1_recv.at[1, k], z_peers[k])
    for k in range(1, 8):
        peer = lax.rem(g + k, 8)
        copy(rows_out.at[peer], rows_in.at[:, :, own_cols], row_send.at[k], row_recv.at[g], (dp, peer))

    sum_a = ga[y].astype(F32)
    sum_b = gb[z].astype(F32)
    for k in range(1, SIDE):
        arrived(ra.at[k], r1_recv.at[0, k])
        sum_a = sum_a + ra[k].astype(F32)
        arrived(rb.at[k], r1_recv.at[1, k])
        sum_b = sum_b + rb[k].astype(F32)
    for j in range(SIDE):
        sa[j] = sum_a[8 * (j // 4) : 8 * (j // 4) + 8, 128 * (j % 4) : 128 * (j % 4) + 128]
    sb[...] = sum_b.reshape(SIDE, 8, COLS)
    for k in range(1, SIDE):
        copy(sa.at[z_at[k]], qa.at[k], r2_send.at[0, k], r2_recv.at[0, k], z_peers[k])
        copy(sb.at[y_at[k]], qb.at[k], r2_send.at[1, k], r2_recv.at[1, k], y_peers[k])

    sum_a = sa[z]
    sum_b = sb[y]
    for k in range(1, SIDE):
        arrived(qa.at[k], r2_recv.at[0, k])
        sum_a = sum_a + qa[k]
        arrived(qb.at[k], r2_recv.at[1, k])
        sum_b = sum_b + qb[k]
    systems = SIDE * SIDE
    fa[z] = sum_a * (scale / math.sqrt(systems * ATOMS))
    fb[y] = sum_b * (16.0 / math.sqrt(systems * 8 * EDGES))
    for k in range(1, SIDE):
        copy(fa.at[z], fa.at[z], r3_send.at[0, k], r3_recv.at[0, z], z_peers[k])
        copy(fb.at[y], fb.at[y], r3_send.at[1, k], r3_recv.at[1, y], y_peers[k])

    for k in range(1, 8):
        peer = lax.rem(g + k, 8)
        peer_cols = pl.ds(pl.multiple_of(peer * COLS, COLS), COLS)
        arrived(rows_in.at[:, :, peer_cols], row_recv.at[peer])
    update = dot(rows_in[0], ow_ref[...]) * scale
    updated_ref[0] = (atoms_ref[0].astype(F32) + update[:OWN]).astype(BF16)
    pushed = dot_nt(rows_in[1], sw_ref[...])
    grad_atoms_ref[0] = (cot_ref[0].astype(F32) + pushed[:OWN]).astype(BF16)

    for k in range(1, SIDE):
        arrived(fa.at[z_at[k]], r3_recv.at[0, z_at[k]])
        arrived(fb.at[y_at[k]], r3_recv.at[1, y_at[k]])
    halves = [jnp.concatenate([fa[4 * h + j] for j in range(4)], axis=1) for h in range(2)]
    out1[g, y] = jnp.concatenate(halves, axis=0).astype(BF16)
    out2[g, z] = fb[...].reshape(64, COLS).astype(BF16)
    for k in range(1, SIDE):
        copy(out1.at[g, y], out1.at[g, y], r4_send.at[0, k], r4_recv.at[0, y], y_peers[k])
        copy(out2.at[g, z], out2.at[g, z], r4_send.at[1, k], r4_recv.at[1, z], z_peers[k])
    for k in range(1, SIDE):
        arrived(out1.at[g, y_at[k]], r4_recv.at[0, y_at[k]])
        arrived(out2.at[g, z_at[k]], r4_recv.at[1, z_at[k]])

    right, left, far = (lax.rem(x + k, 4) for k in (1, 3, 2))
    to_right, to_left, to_other = (dp, 2 * right + core), (dp, 2 * left + core), (dp, 2 * x + other)
    g_right, g_left, g_far = 2 * right + core, 2 * left + core, 2 * far + core

    def pass_on(out, sem, block, slot, device):
        copy(out.at[block], out.at[block], x_send.at[sem, slot], x_recv.at[sem, slot], device)

    def swap(out, sem, block, slot):
        copy(out.at[block], out.at[block], c_send.at[sem, slot], c_recv.at[sem, slot], to_other)

    pass_on(out1, 0, g, 0, to_right)
    pass_on(out2, 1, g, 1, to_left)
    pass_on(out1, 0, g, 1, to_left)
    pass_on(out2, 1, g, 0, to_right)
    swap(out1, 0, g, 0)
    swap(out2, 1, g, 0)
    arrived(out1.at[g_left], x_recv.at[0, 0])
    pass_on(out1, 0, g_left, 2, to_right)
    arrived(out2.at[g_right], x_recv.at[1, 1])
    pass_on(out2, 1, g_right, 2, to_left)
    swap(out1, 0, g_left, 1)
    swap(out2, 1, g_right, 2)
    arrived(out1.at[g_right], x_recv.at[0, 1])
    swap(out1, 0, g_right, 2)
    arrived(out2.at[g_left], x_recv.at[1, 0])
    swap(out2, 1, g_left, 1)
    arrived(out1.at[g_far], x_recv.at[0, 2])
    swap(out1, 0, g_far, 3)
    arrived(out2.at[g_far], x_recv.at[1, 2])
    swap(out2, 1, g_far, 3)
    for slot, block in enumerate((x, left, right, far)):
        arrived(out1.at[2 * block + other], c_recv.at[0, slot])
        arrived(out2.at[2 * block + other], c_recv.at[1, slot])
    for c in sends:
        c.wait_send()


def local(*args):
    vmem = pl.BlockSpec(memory_space=pltpu.VMEM)
    smem = pl.BlockSpec(memory_space=pltpu.SMEM)
    dma = pltpu.SemaphoreType.DMA
    updated, grad_atoms, out1, out2 = pl.pallas_call(
        body,
        out_shape=(
            jax.ShapeDtypeStruct((1, OWN, DA), BF16),
            jax.ShapeDtypeStruct((1, OWN, DA), BF16),
            jax.ShapeDtypeStruct((8, SIDE, 16, DA), BF16),
            jax.ShapeDtypeStruct((8, SIDE, 64, COLS), BF16),
        ),
        in_specs=[vmem] * 6 + [smem] + [vmem] * 3,
        out_specs=(vmem,) * 4,
        scratch_shapes=[
            pltpu.VMEM((8, SLOT, DA), BF16),
            pltpu.VMEM((2, ATOMS, DA), BF16),
            pltpu.VMEM((ATOMS, DE), BF16),
            pltpu.VMEM((EDGES, DA), BF16),
            pltpu.VMEM((EDGES, ATOMS), BF16),
            pltpu.VMEM((ATOMS, EDGES), BF16),
            pltpu.VMEM((ATOMS, EDGES), BF16),
            pltpu.VMEM((EDGES, 8), F32),
            pltpu.VMEM((EDGES, 2 * COLS), BF16),
            pltpu.VMEM((EDGES, 2 * COLS), BF16),
            pltpu.VMEM((4, 2, 2, ATOMS, COLS), BF16),
            pltpu.VMEM((8, 2, ATOMS, COLS), BF16),
            pltpu.VMEM((8, 2, PAD, COLS), BF16),
            pltpu.VMEM((2, PAD, DE), BF16),
            pltpu.VMEM((SIDE, 16, DA), BF16),
            pltpu.VMEM((SIDE, 64, COLS), BF16),
            pltpu.VMEM((SIDE, 16, DA), BF16),
            pltpu.VMEM((SIDE, 64, COLS), BF16),
            pltpu.VMEM((SIDE, 8, COLS), F32),
            pltpu.VMEM((SIDE, 8, COLS), F32),
            pltpu.VMEM((SIDE, 8, COLS), F32),
            pltpu.VMEM((SIDE, 8, COLS), F32),
            pltpu.VMEM((SIDE, 8, COLS), F32),
            pltpu.VMEM((SIDE, 8, COLS), F32),
            dma((8,)),
            dma((8,)),
            dma((8,)),
            dma((8,)),
            dma((8,)),
            dma((8,)),
            dma((2, SIDE)),
            dma((2, SIDE)),
            dma((2, SIDE)),
            dma((2, SIDE)),
            dma((2, SIDE)),
            dma((2, SIDE)),
            dma((2, SIDE)),
            dma((2, SIDE)),
            dma((2, 3)),
            dma((2, 3)),
            dma((2, 4)),
            dma((2, 4)),
        ],
        compiler_params=pltpu.CompilerParams(
            collective_id=0, has_side_effects=True, vmem_limit_bytes=48 * 1024 * 1024
        ),
    )(*args)
    grad_output = out1.reshape(DE, DA)
    grad_source = out2.reshape(8, DA, COLS).transpose(1, 0, 2).reshape(DA, DE)
    return updated, grad_atoms, grad_source, grad_output


def solution(mesh):
    rows = P("dp", "graph", None)
    flat = P("dp", "graph")
    return jax.shard_map(
        local,
        mesh=mesh,
        in_specs=(rows, rows, flat, flat, rows, flat, flat, P(), P(), P()),
        out_specs=(rows, rows, P(), P()),
        check_vma=False,
    )
```

time: 410 us -> 79.9 us (0.19)
  waiting for transfers between devices: 335 us -> 0 us
  Pallas kernels: 0 us -> 66.9 us
  blocking collectives: 32.7 us -> 0 us
  matrix products: 18.6 us -> 0 us
  between operations: 14.5 us -> 1.31 us
  local copies, waits for them, and re-layouts: 1.36 us -> 11.3 us
  other arithmetic: 6.33 us -> 0 us
    psum x1 -> x0, waiting for transfers between devices: 289 us -> none  [local(): source_total, out_total = lax.psum((source_term, out_term), ('dp', 'graph'))]
    pallas_call x0 -> x1, Pallas kernels: none -> 66.9 us  [local(): pl.pallas_call(body, out_shape=(jax.ShapeDtypeStruct((1, OWN, DA), BF16),...]
    reduce_scatter x2 -> x0, waiting for transfers between devices: 45.9 us -> none  [the longest x1 35.4 us: local(): lax.psum_scatter(pushed_part, 'graph', scatter_dimension=0, tiled=True)]
    all_gather x2 -> x0, blocking collectives: 32.7 us -> none  [the longest x1 19.7 us: local(): embed_full = lax.all_gather(embed, 'graph', axis=0, tiled=True)]
    dot_general x10 -> x0, matrix products: 18.6 us -> none  [the longest x4 10.7 us: contract_rows(): lax.dot_general(left, right, (((0,), (0,)), ((), ())), preferred_element_...]
    unnamed x18 -> x21, local copies, waits for them, and re-layouts: 1.36 us -> 10 us
    convert_element_type x2 -> x0, other arithmetic: 4.23 us -> none  [the longest x1 2.96 us: local(): grad_source = (source_total * source_factor).astype(jnp.bfloat16)]
  transfers between devices with their start and end apart: 3 -> 0, of which waited for: 3 -> 0; matrix products, arithmetic and copies ran while one was open for 4% -> 0% of each run, Pallas kernels for 0% -> 0%
where the time goes in v1:
time: 79.9 us; the launch traced here: 79.5 us
  Pallas kernels  66.9 us (84%)
  local copies, waits for them, and re-layouts  11.3 us (14%)
  between operations  1.31 us (2%)
    pallas_call x1, Pallas kernels, local(): pl.pallas_call(body, out_shape=(jax.ShapeDtypeStruct((1, OWN, DA), BF16),...  66.9 us
    unnamed x21, local copies, waits for them, and re-layouts  10 us

profile of v1, /device:TPU:1, one launch (start us, length us, event | category | flops | bytes accessed | tf_op | source)
XLA Modules:
  0.0 79.5 jit_solution(14386312456578724123)
XLA Ops:
  1.3 0.0 copy-start
  1.3 1.2 %copy-done = bf16[512,1024]{1,0:T(8,128)(2,1)S(1)} copy-done((bf16[512,1024]{1,0:T(8,128)(2,1)S(1)}, bf16[512,1024]{1,0:T(8,128)(2,1)}, u32[]{:S(2)}) %copy-start) | copy-done | bytes 1048600
  2.5 0.0 copy-start.1
  2.5 1.2 %copy-done.1 = bf16[1024,512]{1,0:T(8,128)(2,1)S(1)} copy-done((bf16[1024,512]{1,0:T(8,128)(2,1)S(1)}, bf16[1024,512]{1,0:T(8,128)(2,1)}, u32[]{:S(2)}) %copy-start.1) | copy-done | bytes 1048600
  3.7 0.0 copy-start.2
  3.7 0.9 %copy-done.2 = bf16[128,1024]{1,0:T(8,128)(2,1)S(1)} copy-done((bf16[128,1024]{1,0:T(8,128)(2,1)S(1)}, bf16[128,1024]{1,0:T(8,128)(2,1)}, u32[]{:S(2)}) %copy-start.2) | copy-done | bytes 262168
  4.7 0.0 copy-start.3
  4.7 0.9 %copy-done.3 = bf16[1,512,128]{2,1,0:T(8,128)(2,1)S(1)} copy-done((bf16[1,512,128]{2,1,0:T(8,128)(2,1)S(1)}, bf16[1,512,128]{2,1,0:T(8,128)(2,1)}, u32[]{:S(2)}) %copy-start.3) | copy-done | bytes 131096
  5.6 0.0 copy-start.4
  5.6 0.7 copy-done.4
  6.3 0.0 copy-start.5
  6.3 0.7 copy-done.5
  7.1 0.0 copy-start.6
  7.1 0.7 copy-done.6
  7.7 0.0 copy-start.7
  7.7 0.7 copy-done.7
  8.4 0.0 copy-start.8
  8.4 0.7 copy-done.8
  9.1 66.9 %shard_map.129 = (bf16[1,24,512]{2,1,0:T(8,128)(2,1)S(1)}, bf16[1,24,512]{2,1,0:T(8,128)(2,1)S(1)}, bf16[8,8,16,512]{3,2,1,0:T(8,128)(2,1)S(1)}, bf16[8,8,64,128]{3,2,1,0:T(8,128)(2,1)S(1)}) custom-call(bf16[1,24,512]{2,1,0:T(8,128)(2,1)S(1)} %copy-done.4, bf16[1,24,512]{2,1,0:T(8,128)(2,1)S(1)} %copy-done.5, s32[1,512]{1,0:T(1,128)S(1)} %copy-done.6, ...), custom_call_target="tpu_custom_call" | custom-call | tf_op jit(solution)/shard_map/pallas_call | solution.py:309
  76.0 1.3 %copy.17 = bf16[8,64,8,128]{3,2,0,1:T(8,128)(2,1)} copy(bf16[8,64,8,128]{3,2,1,0:T(8,128)(2,1)S(1)} %bitcast.9) | data formatting | bytes 2097152 | tf_op jit(solution)/shard_map/reshape | solution.py:368
  77.3 0.6 copy.22
  77.9 0.6 copy.23
  78.5 1.0 %copy.24 = bf16[1024,512]{1,0:T(8,128)(2,1)} copy(bf16[1024,512]{1,0:T(8,128)(2,1)S(1)} %bitcast.8) | data formatting | bytes 2097152
Async XLA Ops:
  1.3 1.2 %copy-start = (bf16[512,1024]{1,0:T(8,128)(2,1)S(1)}, bf16[512,1024]{1,0:T(8,128)(2,1)}, u32[]{:S(2)}) copy-start(bf16[512,1024]{1,0:T(8,128)(2,1)} %sw_ref.1) | copy-start | bytes 3145732
  2.5 1.2 %copy-start.1 = (bf16[1024,512]{1,0:T(8,128)(2,1)S(1)}, bf16[1024,512]{1,0:T(8,128)(2,1)}, u32[]{:S(2)}) copy-start(bf16[1024,512]{1,0:T(8,128)(2,1)} %ow_ref.1) | copy-start | bytes 3145732
  3.7 0.9 %copy-start.2 = (bf16[128,1024]{1,0:T(8,128)(2,1)S(1)}, bf16[128,1024]{1,0:T(8,128)(2,1)}, u32[]{:S(2)}) copy-start(bf16[128,1024]{1,0:T(8,128)(2,1)} %rw_ref.1) | copy-start | bytes 786436
  4.7 0.9 %copy-start.3 = (bf16[1,512,128]{2,1,0:T(8,128)(2,1)S(1)}, bf16[1,512,128]{2,1,0:T(8,128)(2,1)}, u32[]{:S(2)}) copy-start(bf16[1,512,128]{2,1,0:T(8,128)(2,1)} %radial_ref.1) | copy-start | bytes 393220
  5.6 0.7 copy-start.4
  6.3 0.7 copy-start.5
  7.1 0.7 copy-start.6
  7.7 0.7 copy-start.7
  8.4 0.7 copy-start.8

commit v2 on v1

--- a/solution.py
+++ b/solution.py
@@ -36,63 +36,58 @@
 
 
 def body(
-    atoms_ref,
-    cot_ref,
-    src_ref,
-    dst_ref,
-    radial_ref,
-    env_ref,
     count_ref,
-    sw_ref,
-    rw_ref,
-    ow_ref,
-    updated_ref,
-    grad_atoms_ref,
-    out1,
-    out2,
-    full,
-    atoms_s,
-    back_s,
-    gathered_s,
-    hot_dst_s,
-    hott_src_s,
-    hott_dst_s,
-    cols_s,
-    msg_s,
-    dpre_s,
-    stage,
-    recv,
-    rows_out,
-    rows_in,
-    ga,
-    gb,
-    ra,
-    rb,
-    sa,
-    sb,
-    qa,
-    qb,
-    fa,
-    fb,
-    full_send,
-    full_recv,
-    rs_send,
-    rs_recv,
-    row_send,
-    row_recv,
-    r1_send,
-    r1_recv,
-    r2_send,
-    r2_recv,
-    r3_send,
-    r3_recv,
-    r4_send,
-    r4_recv,
-    x_send,
-    x_recv,
-    c_send,
-    c_recv,
+    *refs,
 ):
+    inputs, refs = refs[:9], refs[9:]
+    updated_ref, grad_atoms_ref, out1, out2 = refs[:4]
+    held = refs[4:13]
+    atoms_ref, cot_ref, src_ref, dst_ref, radial_ref, env_ref, sw_ref, rw_ref, ow_ref = held
+    (
+        full,
+        atoms_s,
+        back_s,
+        gathered_s,
+        hot_dst_s,
+        hott_src_s,
+        hott_dst_s,
+        cols_s,
+        msg_s,
+        dpre_s,
+        stage,
+        recv,
+        rows_out,
+        rows_in,
+        ga,
+        gb,
+        ra,
+        rb,
+        sa,
+        sb,
+        qa,
+        qb,
+        fa,
+        fb,
+        full_send,
+        full_recv,
+        rs_send,
+        rs_recv,
+        row_send,
+        row_recv,
+        r1_send,
+        r1_recv,
+        r2_send,
+        r2_recv,
+        r3_send,
+        r3_recv,
+        r4_send,
+        r4_recv,
+        x_send,
+        x_recv,
+        c_send,
+        c_recv,
+        load_sem,
+    ) = refs[13:]
     dp = lax.axis_index("dp")
     g = lax.axis_index("graph")
     y, z = lax.div(dp, SIDE), lax.rem(dp, SIDE)
@@ -100,6 +95,9 @@
     other = 1 - core
     scale = math.sqrt(OWN / EDGES)
     sends = []
+    loads = [pltpu.make_async_copy(a, b, load_sem.at[i]) for i, (a, b) in enumerate(zip(inputs, held))]
+    for load in loads:
+        load.start()
 
     def copy(src, dst, send, recv_sem, device):
         c = pltpu.make_async_remote_copy(
@@ -123,11 +121,15 @@
     for peer in graph_peers + y_peers[1:] + z_peers[1:]:
         pl.semaphore_signal(barrier, inc=1, device_id=peer, device_id_type=MESH)
 
+    loads[0].wait()
+    loads[1].wait()
     full[g] = jnp.concatenate([atoms_ref[0], cot_ref[0]], axis=0)
     pl.semaphore_wait(barrier, 21)
     for k in range(1, 8):
         copy(full.at[g], full.at[g], full_send.at[k], full_recv.at[g], graph_peers[k - 1])
 
+    for i in (2, 3, 5):
+        loads[i].wait()
     src_row = src_ref[...]
     dst_row = dst_ref[...]
     slots = lax.broadcasted_iota(jnp.int32, (1, EDGES), 1)
@@ -152,6 +154,8 @@
     for k in range(1, 8):
         peer = lax.rem(g + k, 8)
         arrived(full.at[peer], full_recv.at[peer])
+    for i in (4, 6, 7, 8):
+        loads[i].wait()
     both = full[...].reshape(8 * SLOT, DA)
     atoms = dot(pick_atoms, both).astype(BF16)
     cot = dot(pick_cot, both).astype(BF16)
@@ -302,21 +306,37 @@
         c.wait_send()
 
 
-def local(*args):
+def place(updated_in, grad_atoms_in, out1, out2, updated, grad_atoms, grad_source, grad_output, sems):
+    copies = [
+        pltpu.make_async_copy(out2.at[i], grad_source.at[:, pl.ds(i * COLS, COLS)], sems.at[i]) for i in range(8)
+    ]
+    copies.append(pltpu.make_async_copy(out1, grad_output, sems.at[8]))
+    copies.append(pltpu.make_async_copy(updated_in, updated, sems.at[9]))
+    copies.append(pltpu.make_async_copy(grad_atoms_in, grad_atoms, sems.at[10]))
+    for c in copies:
+        c.start()
+    for c in copies:
+        c.wait()
+
+
+def local(atoms, cotangent, sources, targets, radial, envelope, edge_counts, source_weight, radial_weight, output_weight):
+    inputs = (atoms, cotangent, sources, targets, radial, envelope, source_weight, radial_weight, output_weight)
+    hbm = pl.BlockSpec(memory_space=pltpu.HBM)
     vmem = pl.BlockSpec(memory_space=pltpu.VMEM)
     smem = pl.BlockSpec(memory_space=pltpu.SMEM)
     dma = pltpu.SemaphoreType.DMA
     updated, grad_atoms, out1, out2 = pl.pallas_call(
         body,
         out_shape=(
-            jax.ShapeDtypeStruct((1, OWN, DA), BF16),
-            jax.ShapeDtypeStruct((1, OWN, DA), BF16),
-            jax.ShapeDtypeStruct((8, SIDE, 16, DA), BF16),
-            jax.ShapeDtypeStruct((8, SIDE, 64, COLS), BF16),
+            pltpu.VMEM((1, OWN, DA), BF16),
+            pltpu.VMEM((1, OWN, DA), BF16),
+            pltpu.VMEM((8, SIDE, 16, DA), BF16),
+            pltpu.VMEM((8, SIDE, 64, COLS), BF16),
         ),
-        in_specs=[vmem] * 6 + [smem] + [vmem] * 3,
+        in_specs=[smem] + [hbm] * 9,
         out_specs=(vmem,) * 4,
-        scratch_shapes=[
+        scratch_shapes=[pltpu.VMEM(a.shape, a.dtype) for a in inputs]
+        + [
             pltpu.VMEM((8, SLOT, DA), BF16),
             pltpu.VMEM((2, ATOMS, DA), BF16),
             pltpu.VMEM((ATOMS, DE), BF16),
@@ -359,14 +379,25 @@
             dma((2, 3)),
             dma((2, 4)),
             dma((2, 4)),
+            dma((9,)),
         ],
         compiler_params=pltpu.CompilerParams(
             collective_id=0, has_side_effects=True, vmem_limit_bytes=48 * 1024 * 1024
         ),
-    )(*args)
-    grad_output = out1.reshape(DE, DA)
-    grad_source = out2.reshape(8, DA, COLS).transpose(1, 0, 2).reshape(DA, DE)
-    return updated, grad_atoms, grad_source, grad_output
+    )(edge_counts, *(pltpu.with_memory_space_constraint(a, pltpu.HBM) for a in inputs))
+    results = (updated, grad_atoms, out1.reshape(DE, DA), out2.reshape(8, DA, COLS))
+    return pl.pallas_call(
+        place,
+        out_shape=(
+            jax.ShapeDtypeStruct((1, OWN, DA), BF16),
+            jax.ShapeDtypeStruct((1, OWN, DA), BF16),
+            jax.ShapeDtypeStruct((DA, DE), BF16),
+            jax.ShapeDtypeStruct((DE, DA), BF16),
+        ),
+        in_specs=[vmem] * 4,
+        out_specs=(hbm,) * 4,
+        scratch_shapes=[dma((11,))],
+    )(*(pltpu.with_memory_space_constraint(a, pltpu.VMEM) for a in results))
 
 
 def solution(mesh):

time: 79.9 us -> 70.4 us (0.88)
  local copies, waits for them, and re-layouts: 11.3 us -> 0 us
  Pallas kernels: 66.9 us -> 69 us
    unnamed x21 -> x0, local copies, waits for them, and re-layouts: 10 us -> none
    pallas_call x1 -> x2, Pallas kernels: 66.9 us -> 69 us  [the longest x1 67.6 us: local(): pl.pallas_call(body, out_shape=(pltpu.VMEM((1, OWN, DA), BF16), pltpu.VME...]
    reshape x1 -> x0, local copies, waits for them, and re-layouts: 1.27 us -> none  [local(): grad_source = out2.reshape(8, DA, COLS).transpose(1, 0, 2).reshape(DA, DE)]
where the time goes in v2:
time: 70.4 us; the launch traced here: 70.3 us
  Pallas kernels  69 us (98%)
  between operations  1.29 us (2%)
    pallas_call x1, Pallas kernels, local(): pl.pallas_call(body, out_shape=(pltpu.VMEM((1, OWN, DA), BF16), pltpu.VME...  67.6 us
    pallas_call x1, Pallas kernels, local(): pl.pallas_call(place, out_shape=(jax.ShapeDtypeStruct((1, OWN, DA), BF16)...  1.42 us

profile of v2, /device:TPU:1, one launch (start us, length us, event | category | flops | bytes accessed | tf_op | source)
XLA Modules:
  0.0 70.3 jit_solution(18271220294295031920)
XLA Ops:
  1.3 67.6 %shard_map.129 = (bf16[1,24,512]{2,1,0:T(8,128)(2,1)S(1)}, bf16[1,24,512]{2,1,0:T(8,128)(2,1)S(1)}, bf16[8,8,16,512]{3,2,1,0:T(8,128)(2,1)S(1)}, bf16[8,8,64,128]{3,2,1,0:T(8,128)(2,1)S(1)}) custom-call(s32[1,1]{1,0:T(1,128)S(6)} %copy.14.count_ref, bf16[1,24,512]{2,1,0:T(8,128)(2,1)} %refs_0_.1, bf16[1,24,512]{2,1,0:T(8,128)(2,1)} %refs_1_.1, ...), custom_call_target="tpu_custom_call" | custom-call | tf_op jit(solution)/shard_map/pallas_call | solution.py:328
  68.9 1.4 %shard_map.130 = (bf16[1,24,512]{2,1,0:T(8,128)(2,1)}, bf16[1,24,512]{2,1,0:T(8,128)(2,1)}, bf16[512,1024]{1,0:T(8,128)(2,1)}, bf16[1024,512]{1,0:T(8,128)(2,1)}) custom-call(bf16[1,24,512]{2,1,0:T(8,128)(2,1)S(1)} %get-tuple-element.8.updated_in, bf16[1,24,512]{2,1,0:T(8,128)(2,1)S(1)} %get-tuple-element.9.grad_atoms_in, bf16[1024,512]{1,0:T(8,128)(2,1)S(1)} %bitcast.2, ...), custom_call_target="tpu_custom_call" | custom-call | tf_op jit(solution)/shard_map/pallas_call | solution.py:389

commit v3 on v0

v3 whole, which is shorter than its diff:
```python
import math

import jax
import jax.numpy as jnp
from jax import lax
from jax.experimental import pallas as pl
from jax.experimental.pallas import tpu as pltpu
from jax.sharding import PartitionSpec as P

MESH = pl.DeviceIdType.MESH
F32 = jnp.float32
BF16 = jnp.bfloat16

OWN = 24
ATOMS = 192
EDGES = 512
DA = 512
DE = 1024
NR = 128
PAD = 32
REST = 2 * OWN - PAD
COLS = 128
SIDE = 8
NEAR = (0, 1, 7, 2, 6, 3, 5, 4)
NEAR_X = (0, 1, 3, 2)
GROUPS = ((1, 3), (3, 5), (5, 8))
GROUPS_X = ((1, 3), (3, 4))


def dot(left, right):
    return jnp.dot(left, right, preferred_element_type=F32)


def dot_nt(left, right):
    return lax.dot_general(left, right, (((1,), (1,)), ((), ())), preferred_element_type=F32)


def dot_tn(left, right):
    return lax.dot_general(left, right, (((0,), (0,)), ((), ())), preferred_element_type=F32)


def hot(hit):
    return hit.astype(F32).astype(BF16)


def by_owner(index):
    return (index * 683) >> 14


def body(count_ref, *refs):
    inputs, refs = refs[:9], refs[9:]
    updated_ref, grad_atoms_ref, out1, out2 = refs[:4]
    (
        atoms_ref,
        cot_ref,
        src_ref,
        dst_ref,
        env_ref,
        ow_ref,
        left_s,
        right_s,
        full1,
        full2,
        atoms_s,
        atoms_t,
        cot_s,
        back_s,
        hot_src_s,
        hot_dst_s,
        hott_src_s,
        hott_dst_s,
        grow_s,
        cols_s,
        weight_s,
        pre_s,
        pulled_s,
        msg_s,
        dpre_s,
        keep,
        swap_out,
        swap_in,
        x_out,
        x_in,
        rows_out,
        rows_in,
        ga,
        gb,
        ra,
        rb,
        pa,
        pb,
        a1,
        a2,
        b1,
        b2,
        load_sem,
        full_send,
        full_recv,
        rs_send,
        rs_recv,
        row_send,
        row_recv,
        sum_send,
        sum_recv,
        g_send,
        near_recv,
        far_recv,
        core_recv,
    ) = refs[4:]
    dp = lax.axis_index("dp")
    g = lax.axis_index("graph")
    y, z = lax.div(dp, SIDE), lax.rem(dp, SIDE)
    x, core = lax.div(g, 2), lax.rem(g, 2)
    other = 1 - core
    scale = math.sqrt(OWN / EDGES)
    me = (dp, g)

    def send(src, dst, send_sem, recv_sem, device):
        pltpu.make_async_remote_copy(
            src_ref=src, dst_ref=dst, send_sem=send_sem, recv_sem=recv_sem, device_id=device, device_id_type=MESH
        ).start()

    def arrived(dst, sem):
        pltpu.make_async_remote_copy(
            src_ref=dst, dst_ref=dst, send_sem=sem, recv_sem=sem, device_id=me, device_id_type=MESH
        ).wait_recv()

    def sent(src, sem):
        pltpu.make_async_remote_copy(
            src_ref=src, dst_ref=src, send_sem=sem, recv_sem=sem, device_id=me, device_id_type=MESH
        ).wait_send()

    y_at = [lax.rem(y + k, SIDE) for k in range(SIDE)]
    z_at = [lax.rem(z + k, SIDE) for k in range(SIDE)]
    x_at = [lax.rem(x + k, 4) for k in range(4)]
    y_peer = [(y_at[k] * SIDE + z, g) for k in range(SIDE)]
    z_peer = [(y * SIDE + z_at[k], g) for k in range(SIDE)]
    x_peer = [(dp, 2 * x_at[k] + core) for k in range(4)]
    x_peer_other = [(dp, 2 * x_at[k] + other) for k in range(4)]
    sibling = x_peer_other[0]
    graph_peers = [x_peer[2], x_peer_other[2], x_peer[1], x_peer_other[1], x_peer[3], x_peer_other[3], sibling]

    barrier = pltpu.get_barrier_semaphore()
    for k in reversed(NEAR[1:]):
        for peer in (y_peer[k], z_peer[k]):
            pl.semaphore_signal(barrier, inc=1, device_id=peer, device_id_type=MESH)
    for peer in graph_peers:
        pl.semaphore_signal(barrier, inc=1, device_id=peer, device_id_type=MESH)

    places = (
        atoms_ref,
        cot_ref,
        src_ref,
        dst_ref,
        left_s.at[:, pl.ds(0, NR)],
        env_ref,
        right_s.at[pl.ds(NR, DA)],
        right_s.at[pl.ds(0, NR)],
        ow_ref,
    )
    loads = []
    for i, place in enumerate(places):
        held = inputs[i].at[0] if i == 4 else inputs[i]
        loads.append(pltpu.make_async_copy(held, place, load_sem.at[i]))
        loads[i].start()

    loads[0].wait()
    loads[1].wait()
    stacked = jnp.concatenate([atoms_ref[0], cot_ref[0]], axis=0)
    full1[g] = stacked[:PAD]
    full2[g] = stacked[PAD:]
    pl.semaphore_wait(barrier, 21)
    for peer in graph_peers:
        send(full1.at[g], full1.at[g], full_send.at[0], full_recv.at[0, g], peer)
    for peer in graph_peers:
        send(full2.at[g], full2.at[g], full_send.at[1], full_recv.at[1, g], peer)

    for i in (2, 3, 5):
        loads[i].wait()
    src_row = src_ref[...]
    dst_row = dst_ref[...]
    slots = lax.broadcasted_iota(jnp.int32, (1, EDGES), 1)
    live = (slots < count_ref[0, 0]).astype(F32)
    src_padded = src_row + (PAD - OWN) * by_owner(src_row)
    table = jnp.concatenate(
        [src_padded.astype(F32), dst_row.astype(F32), env_ref[...] * live, jnp.zeros((5, EDGES), F32)], axis=0
    )
    cols_s[...] = table.T
    hot_src_s[...] = hot(lax.broadcasted_iota(jnp.int32, (EDGES, 8 * PAD), 1).astype(F32) == cols_s[:, 0:1])
    hot_dst_s[...] = hot(lax.broadcasted_iota(jnp.int32, (EDGES, ATOMS), 1).astype(F32) == cols_s[:, 1:2])
    weight_s[...] = jnp.broadcast_to(cols_s[:, 2:3], (EDGES, COLS))
    atom_rows = lax.broadcasted_iota(jnp.int32, (ATOMS, EDGES), 0)
    hott_src_s[...] = hot(atom_rows == src_row)
    hott_dst_s[...] = hot(atom_rows == dst_row)
    at1_r = lax.broadcasted_iota(jnp.int32, (ATOMS, 8 * PAD), 0)
    at1_c = lax.broadcasted_iota(jnp.int32, (ATOMS, 8 * PAD), 1)
    at1 = at1_r + (PAD - OWN) * by_owner(at1_r)
    pick_atoms = hot(at1_c == at1)
    inner = at1_r - OWN * by_owner(at1_r)
    pick_cot1 = hot((at1_c == at1 + OWN) & (inner < PAD - OWN))
    at2_r = lax.broadcasted_iota(jnp.int32, (ATOMS, 8 * REST), 0)
    at2_c = lax.broadcasted_iota(jnp.int32, (ATOMS, 8 * REST), 1)
    owner2 = by_owner(at2_r)
    inner2 = at2_r - OWN * owner2
    pick_cot2 = hot((at2_c == owner2 * REST + inner2 - (PAD - OWN)) & (inner2 >= PAD - OWN))
    for i in (4, 6, 7, 8):
        loads[i].wait()

    for peer in graph_peers:
        arrived(full1.at[peer[1]], full_recv.at[0, peer[1]])
    both = full1[...].reshape(8 * PAD, DA)
    left_s[:, NR:] = dot(hot_src_s[...], both).astype(BF16)
    for peer in graph_peers:
        arrived(full2.at[peer[1]], full_recv.at[1, peer[1]])
    cot = (dot(pick_cot1, both) + dot(pick_cot2, full2[...].reshape(8 * REST, DA))).astype(BF16)
    cot_s[...] = cot
    back_s[...] = (dot_nt(cot, ow_ref[...]) * scale).astype(BF16)

    def pass_x(dx):
        arrived(swap_in.at[dx], rs_recv.at[0, dx])
        x_out[dx] = (keep[dx] + swap_in[dx].astype(F32)).astype(BF16)
        send(x_out.at[dx], x_in.at[dx], rs_send.at[1, dx], rs_recv.at[1, dx], x_peer[dx])

    before = None
    for dx in (2, 1, 3, 0):
        cols = pl.ds(pl.multiple_of(x_at[dx] * 2 * COLS, 2 * COLS), 2 * COLS)
        pre_s[...] = dot(left_s[...], right_s[:, cols])
        pulled_s[...] = dot(hot_dst_s[...], back_s[:, cols])
        for r in range(8):
            rows = slice(r * 64, (r + 1) * 64)
            pre = pre_s[rows, :]
            weight = jnp.concatenate([weight_s[rows, :]] * 2, axis=1)
            sigma = 0.5 * jnp.tanh(0.5 * pre) + 0.5
            silu = pre * sigma
            msg_s[rows, :] = (silu * weight).astype(BF16)
            slope = sigma + silu * (1.0 - sigma)
            dpre_s[rows, :] = (pulled_s[rows, :] * weight * slope).astype(BF16)
        for j, (picks, terms) in enumerate(((hott_dst_s, msg_s), (hott_src_s, dpre_s))):
            part = dot(picks[...], terms[...])
            low, high = part[:, :COLS], part[:, COLS:]
            keep[dx, j] = jnp.where(core == 0, low, high)
            swap_out[dx, j] = jnp.where(core == 0, high, low).astype(BF16)
        send(swap_out.at[dx], swap_in.at[dx], rs_send.at[0, dx], rs_recv.at[0, dx], sibling)
        if before:
            pass_x(before)
        before = dx

    atoms_s[...] = dot(pick_atoms, both).astype(BF16)
    atoms_t[...] = atoms_s[...].astype(F32).T.astype(BF16)
    grow_r = lax.broadcasted_iota(jnp.int32, (8 * PAD, ATOMS), 0)
    grow_c = lax.broadcasted_iota(jnp.int32, (8 * PAD, ATOMS), 1)
    inner = grow_r & (PAD - 1)
    grow_s[...] = hot((inner < OWN) & (grow_c == (grow_r >> 5) * OWN + inner))
    arrived(swap_in.at[0], rs_recv.at[0, 0])
    total = keep[0] + swap_in[0].astype(F32)
    for dx in (2, 1, 3):
        arrived(x_in.at[dx], rs_recv.at[1, dx])
        total = total + x_in[dx].astype(F32)
    sums = total.astype(BF16)
    summed, dsum = sums[0], sums[1]

    ga[...] = dot_tn(summed, cot_s[...]).astype(BF16).reshape(SIDE, 16, DA)
    gb[...] = dot(atoms_t[...], dsum).astype(BF16).reshape(SIDE, 64, COLS)
    for k in reversed(NEAR[1:]):
        send(ga.at[y_at[k]], ra.at[k], sum_send.at[0], sum_recv.at[0], y_peer[k])
        send(gb.at[z_at[k]], rb.at[k], sum_send.at[1], sum_recv.at[1], z_peer[k])

    rows_out[:, 0] = dot(grow_s[...], summed).astype(BF16).reshape(8, PAD, COLS)
    rows_out[:, 1] = dot(grow_s[...], dsum).astype(BF16).reshape(8, PAD, COLS)
    own_cols = pl.ds(pl.multiple_of(g * COLS, COLS), COLS)
    rows_in[:, :, own_cols] = rows_out[g]
    for peer in graph_peers:
        send(rows_out.at[peer[1]], rows_in.at[:, :, own_cols], row_send, row_recv.at[g], peer)

    arrived(ra.at[pl.ds(1, 7)], sum_recv.at[0])
    arrived(rb.at[pl.ds(1, 7)], sum_recv.at[1])
    sum_a = ga[y].astype(F32)
    sum_b = gb[z].astype(F32)
    for k in range(1, SIDE):
        sum_a = sum_a + ra[k].astype(F32)
        sum_b = sum_b + rb[k].astype(F32)

    pa[0] = sum_a.astype(BF16)
    pb[0] = sum_b.astype(BF16)
    for k in reversed(NEAR[1:]):
        send(pa.at[0], pa.at[k], sum_send.at[2], sum_recv.at[2], z_peer[k])
        send(pb.at[0], pb.at[k], sum_send.at[3], sum_recv.at[3], y_peer[k])

    for peer in graph_peers:
        peer_cols = pl.ds(pl.multiple_of(peer[1] * COLS, COLS), COLS)
        arrived(rows_in.at[:, :, peer_cols], row_recv.at[peer[1]])
    update = dot(rows_in[0], ow_ref[...]) * scale
    updated_ref[0] = (atoms_ref[0].astype(F32) + update[:OWN]).astype(BF16)
    pushed = dot_nt(rows_in[1], right_s[NR:, :])
    grad_atoms_ref[0] = (cot_ref[0].astype(F32) + pushed[:OWN]).astype(BF16)

    arrived(pa.at[pl.ds(1, 7)], sum_recv.at[2])
    arrived(pb.at[pl.ds(1, 7)], sum_recv.at[3])
    sum_a = pa[z].astype(F32)
    sum_b = pb[y].astype(F32)
    for j in range(1, SIDE):
        sum_a = sum_a + pa[lax.rem(z + SIDE - j, SIDE)].astype(F32)
        sum_b = sum_b + pb[lax.rem(y + SIDE - j, SIDE)].astype(F32)
    systems = SIDE * SIDE
    piece_a = (sum_a * (scale / math.sqrt(systems * ATOMS))).astype(BF16)
    piece_b = (sum_b * (16.0 / math.sqrt(systems * 8 * EDGES))).astype(BF16)
    a1[core, 0, 0] = piece_a[:, : DA // 2]
    a2[core, 0, 0] = piece_a[:, DA // 2 :]
    b1[core, 0, 0] = piece_b[:32]
    b2[core, 0, 0] = piece_b[32:]

    back_to = [[y_peer[(SIDE - k) % SIDE] for k in NEAR], [z_peer[(SIDE - k) % SIDE] for k in NEAR]]
    back_x = [x_peer[(4 - k) % 4] for k in NEAR_X]
    first = ((a1, 0, back_to[0]), (b1, 1, back_to[1]))
    second = ((a2, 2, back_to[0]), (b2, 3, back_to[1]))

    def group_of(s):
        return 0 if s < 3 else 1 if s < 5 else 2

    def pass_first(buf, n, lo, hi):
        for s in (3, 1, 2):
            send(
                buf.at[core, 0, pl.ds(lo, hi - lo)],
                buf.at[core, s, pl.ds(lo, hi - lo)],
                g_send.at[n, 1],
                far_recv.at[n, s - 1],
                back_x[s],
            )

    def pass_second(buf, n, peers, lo, hi):
        for s in range(7, 0, -1):
            send(
                buf.at[core, 0, pl.ds(lo, hi - lo)],
                buf.at[core, s, pl.ds(lo, hi - lo)],
                g_send.at[n, 1],
                far_recv.at[n, group_of(s)],
                peers[s],
            )

    def pass_core(buf, n, slot, lo, hi):
        send(
            buf.at[core, pl.ds(lo, hi - lo)],
            buf.at[core, pl.ds(lo, hi - lo)],
            g_send.at[n, 2],
            core_recv.at[n, slot],
            sibling,
        )

    for buf, n, peers in second:
        for s in (3, 1, 2):
            send(buf.at[core, 0, 0], buf.at[core, 0, s], g_send.at[n, 0], near_recv.at[n, 0 if s < 3 else 1], back_x[s])
    for buf, n, peers in first:
        for s in range(7, 0, -1):
            send(buf.at[core, 0, 0], buf.at[core, 0, s], g_send.at[n, 0], near_recv.at[n, group_of(s)], peers[s])
        pass_first(buf, n, 0, 1)
    for buf, n, peers in second:
        pass_second(buf, n, peers, 0, 1)
    for i in range(3):
        if i < 2:
            lo, hi = GROUPS_X[i]
            for buf, n, peers in second:
                arrived(buf.at[core, 0, pl.ds(lo, hi - lo)], near_recv.at[n, i])
                pass_second(buf, n, peers, lo, hi)
        lo, hi = GROUPS[i]
        for buf, n, peers in first:
            arrived(buf.at[core, 0, pl.ds(lo, hi - lo)], near_recv.at[n, i])
            pass_first(buf, n, lo, hi)
    for buf, n, peers in second + first:
        pass_core(buf, n, 0, 0, 1)

    def store(n, c, xs, ys):
        owner = 2 * x_at[NEAR_X[xs]] + c
        if n in (0, 2):
            piece = a1[c, xs, ys] if n == 0 else a2[c, ys, xs]
            half = slice(0, DA // 2) if n == 0 else slice(DA // 2, DA)
            out1[owner, y_at[NEAR[ys]], :, half] = piece
        else:
            piece = b1[c, xs, ys] if n == 1 else b2[c, ys, xs]
            rows = pl.ds(pl.multiple_of(z_at[NEAR[ys]] * 64 + (0 if n == 1 else 32), 32), 32)
            out2[rows, pl.ds(pl.multiple_of(owner * COLS, COLS), COLS)] = piece

    def store_all(n, c, lo, hi):
        for s in range(lo, hi):
            for t in range(8 if n < 2 else 4):
                if n < 2:
                    store(n, c, s, t)
                else:
                    store(n, c, t, s)

    for buf, n, peers in second + first:
        store_all(n, core, 0, 1)
    parts = []
    for i in range(3):
        for buf, n, peers in second:
            parts.append((buf, n, i, *GROUPS[i]))
        for buf, n, peers in first:
            parts.append((buf, n, i, i + 1, i + 2))
    for buf, n, i, lo, hi in parts:
        arrived(buf.at[core, pl.ds(lo, hi - lo)], far_recv.at[n, i])
        pass_core(buf, n, i + 1, lo, hi)
        store_all(n, core, lo, hi)
    for buf, n, peers in second + first:
        arrived(buf.at[other, pl.ds(0, 1)], core_recv.at[n, 0])
        store_all(n, other, 0, 1)
    for buf, n, i, lo, hi in parts:
        arrived(buf.at[other, pl.ds(lo, hi - lo)], core_recv.at[n, i + 1])
        store_all(n, other, lo, hi)

    for buf, n, peers in first + second:
        sent(buf.at[core, 0, pl.ds(1, 7 if n < 2 else 3)], g_send.at[n, 0])
        sent(buf.at[core, pl.ds(1, 3 if n < 2 else 7)], g_send.at[n, 1])
        sent(buf.at[core], g_send.at[n, 2])
    sent(full1.at[pl.ds(0, 7)], full_send.at[0])
    sent(full2.at[pl.ds(0, 7)], full_send.at[1])
    for dx in range(4):
        sent(swap_out.at[dx], rs_send.at[0, dx])
        if dx:
            sent(x_out.at[dx], rs_send.at[1, dx])
    sent(rows_out.at[pl.ds(0, 7)], row_send)
    sent(ra.at[pl.ds(1, 7)], sum_send.at[0])
    sent(rb.at[pl.ds(1, 7)], sum_send.at[1])
    sent(pa.at[pl.ds(1, 7)], sum_send.at[2])
    sent(pb.at[pl.ds(1, 7)], sum_send.at[3])


def place(*refs):
    sems = refs[8]
    copies = [pltpu.make_async_copy(refs[i], refs[4 + i], sems.at[i]) for i in range(4)]
    for c in copies:
        c.start()
    for c in copies:
        c.wait()


def local(atoms, cotangent, sources, targets, radial, envelope, edge_counts, source_weight, radial_weight, output_weight):
    inputs = (atoms, cotangent, sources, targets, radial, envelope, source_weight, radial_weight, output_weight)
    vmem = pl.BlockSpec(memory_space=pltpu.VMEM)
    smem = pl.BlockSpec(memory_space=pltpu.SMEM)
    hbm = pl.BlockSpec(memory_space=pltpu.HBM)
    dma = pltpu.SemaphoreType.DMA

    def like(a):
        return pltpu.VMEM(a.shape, a.dtype)

    updated, grad_atoms, out1, out2 = pl.pallas_call(
        body,
        out_shape=(
            pltpu.VMEM((1, OWN, DA), BF16),
            pltpu.VMEM((1, OWN, DA), BF16),
            pltpu.VMEM((8, SIDE, 16, DA), BF16),
            pltpu.VMEM((DA, DE), BF16),
        ),
        in_specs=[smem] + [hbm] * 9,
        out_specs=(vmem,) * 4,
        scratch_shapes=[
            like(atoms),
            like(cotangent),
            like(sources),
            like(targets),
            like(envelope),
            like(output_weight),
            pltpu.VMEM((EDGES, NR + DA), BF16),
            pltpu.VMEM((NR + DA, DE), BF16),
            pltpu.VMEM((8, PAD, DA), BF16),
            pltpu.VMEM((8, REST, DA), BF16),
            pltpu.VMEM((ATOMS, DA), BF16),
            pltpu.VMEM((DA, ATOMS), BF16),
            pltpu.VMEM((ATOMS, DA), BF16),
            pltpu.VMEM((ATOMS, DE), BF16),
            pltpu.VMEM((EDGES, 8 * PAD), BF16),
            pltpu.VMEM((EDGES, ATOMS), BF16),
            pltpu.VMEM((ATOMS, EDGES), BF16),
            pltpu.VMEM((ATOMS, EDGES), BF16),
            pltpu.VMEM((8 * PAD, ATOMS), BF16),
            pltpu.VMEM((EDGES, 8), F32),
            pltpu.VMEM((EDGES, COLS), F32),
            pltpu.VMEM((EDGES, 2 * COLS), F32),
            pltpu.VMEM((EDGES, 2 * COLS), F32),
            pltpu.VMEM((EDGES, 2 * COLS), BF16),
            pltpu.VMEM((EDGES, 2 * COLS), BF16),
            pltpu.VMEM((4, 2, ATOMS, COLS), F32),
            pltpu.VMEM((4, 2, ATOMS, COLS), BF16),
            pltpu.VMEM((4, 2, ATOMS, COLS), BF16),
            pltpu.VMEM((4, 2, ATOMS, COLS), BF16),
            pltpu.VMEM((4, 2, ATOMS, COLS), BF16),
            pltpu.VMEM((8, 2, PAD, COLS), BF16),
            pltpu.VMEM((2, PAD, DE), BF16),
            pltpu.VMEM((SIDE, 16, DA), BF16),
            pltpu.VMEM((SIDE, 64, COLS), BF16),
            pltpu.VMEM((SIDE, 16, DA), BF16),
            pltpu.VMEM((SIDE, 64, COLS), BF16),
            pltpu.VMEM((SIDE, 16, DA), BF16),
            pltpu.VMEM((SIDE, 64, COLS), BF16),
            pltpu.VMEM((2, 4, SIDE, 16, DA // 2), BF16),
            pltpu.VMEM((2, SIDE, 4, 16, DA // 2), BF16),
            pltpu.VMEM((2, 4, SIDE, 32, COLS), BF16),
            pltpu.VMEM((2, SIDE, 4, 32, COLS), BF16),
            dma((9,)),
            dma((2,)),
            dma((2, 8)),
            dma((2, 4)),
            dma((2, 4)),
            dma,
            dma((8,)),
            dma((4,)),
            dma((4,)),
            dma((4, 3)),
            dma((4, 3)),
            dma((4, 3)),
            dma((4, 4)),
        ],
        compiler_params=pltpu.CompilerParams(
            collective_id=0, has_side_effects=True, vmem_limit_bytes=48 * 1024 * 1024
        ),
    )(edge_counts, *(pltpu.with_memory_space_constraint(a, pltpu.HBM) for a in inputs))
    results = (updated, grad_atoms, out2, out1.reshape(DE, DA))
    return pl.pallas_call(
        place,
        out_shape=tuple(jax.ShapeDtypeStruct(a.shape, a.dtype) for a in results),
        in_specs=[vmem] * 4,
        out_specs=(hbm,) * 4,
        scratch_shapes=[dma((4,))],
    )(*(pltpu.with_memory_space_constraint(a, pltpu.VMEM) for a in results))


def solution(mesh):
    rows = P("dp", "graph", None)
    flat = P("dp", "graph")
    return jax.shard_map(
        local,
        mesh=mesh,
        in_specs=(rows, rows, flat, flat, rows, flat, flat, P(), P(), P()),
        out_specs=(rows, rows, P(), P()),
        check_vma=False,
    )
```

time: 410 us -> 58.3 us (0.14)
  waiting for transfers between devices: 335 us -> 0 us
  Pallas kernels: 0 us -> 56.9 us
  blocking collectives: 32.7 us -> 0 us
  matrix products: 18.6 us -> 0 us
  between operations: 14.5 us -> 1.29 us
  other arithmetic: 6.33 us -> 0 us
    psum x1 -> x0, waiting for transfers between devices: 289 us -> none  [local(): source_total, out_total = lax.psum((source_term, out_term), ('dp', 'graph'))]
    pallas_call x0 -> x2, Pallas kernels: none -> 56.9 us  [the longest x1 55.5 us: local(): pl.pallas_call(body, out_shape=(pltpu.VMEM((1, OWN, DA), BF16), pltpu.VME...]
    reduce_scatter x2 -> x0, waiting for transfers between devices: 45.9 us -> none  [the longest x1 35.4 us: local(): lax.psum_scatter(pushed_part, 'graph', scatter_dimension=0, tiled=True)]
    all_gather x2 -> x0, blocking collectives: 32.7 us -> none  [the longest x1 19.7 us: local(): embed_full = lax.all_gather(embed, 'graph', axis=0, tiled=True)]
    dot_general x10 -> x0, matrix products: 18.6 us -> none  [the longest x4 10.7 us: contract_rows(): lax.dot_general(left, right, (((0,), (0,)), ((), ())), preferred_element_...]
    convert_element_type x2 -> x0, other arithmetic: 4.23 us -> none  [the longest x1 2.96 us: local(): grad_source = (source_total * source_factor).astype(jnp.bfloat16)]
  transfers between devices with their start and end apart: 3 -> 0, of which waited for: 3 -> 0; matrix products, arithmetic and copies ran while one was open for 4% -> 0% of each run, Pallas kernels for 0% -> 0%
where the time goes in v3:
time: 58.3 us; the launch traced here: 58.1 us
  Pallas kernels  56.9 us (98%)
  between operations  1.29 us (2%)
    pallas_call x1, Pallas kernels, local(): pl.pallas_call(body, out_shape=(pltpu.VMEM((1, OWN, DA), BF16), pltpu.VME...  55.5 us
    pallas_call x1, Pallas kernels, local(): pl.pallas_call(place, out_shape=tuple((jax.ShapeDtypeStruct(a.shape, a.dt...  1.37 us

profile of v3, /device:TPU:1, one launch (start us, length us, event | category | flops | bytes accessed | tf_op | source)
XLA Modules:
  0.0 58.1 jit_solution(2076456939357752402)
XLA Ops:
  1.3 55.5 %shard_map.129 = (bf16[1,24,512]{2,1,0:T(8,128)(2,1)S(1)}, bf16[1,24,512]{2,1,0:T(8,128)(2,1)S(1)}, bf16[8,8,16,512]{3,2,1,0:T(8,128)(2,1)S(1)}, bf16[512,1024]{1,0:T(8,128)(2,1)S(1)}) custom-call(s32[1,1]{1,0:T(1,128)S(6)} %copy.14.count_ref, bf16[1,24,512]{2,1,0:T(8,128)(2,1)} %refs_0_.1, bf16[1,24,512]{2,1,0:T(8,128)(2,1)} %refs_1_.1, s32[1,512]{1,0:T(1,128)} %refs_2_.1, ...), custom_call_target="tpu_custom_call" | custom-call | tf_op jit(solution)/shard_map/pallas_call | solution.py:445
  56.8 1.4 %shard_map.130 = (bf16[1,24,512]{2,1,0:T(8,128)(2,1)}, bf16[1,24,512]{2,1,0:T(8,128)(2,1)}, bf16[512,1024]{1,0:T(8,128)(2,1)}, bf16[1024,512]{1,0:T(8,128)(2,1)}) custom-call(bf16[1,24,512]{2,1,0:T(8,128)(2,1)S(1)} %get-tuple-element.8.refs_0_, bf16[1,24,512]{2,1,0:T(8,128)(2,1)S(1)} %get-tuple-element.9.refs_1_, ...), custom_call_target="tpu_custom_call" | custom-call | tf_op jit(solution)/shard_map/pallas_call | solution.py:517

commit v4 on v3

--- a/solution.py
+++ b/solution.py
@@ -17,8 +17,8 @@
 DA = 512
 DE = 1024
 NR = 128
+SLOT = 2 * OWN
 PAD = 32
-REST = 2 * OWN - PAD
 COLS = 128
 SIDE = 8
 NEAR = (0, 1, 7, 2, 6, 3, 5, 4)
@@ -57,30 +57,23 @@
         dst_ref,
         env_ref,
         ow_ref,
-        left_s,
-        right_s,
-        full1,
-        full2,
+        rw_ref,
+        sw_ref,
+        basis,
+        table,
+        full,
         atoms_s,
         atoms_t,
         cot_s,
+        rows_s,
         back_s,
         hot_src_s,
         hot_dst_s,
         hott_src_s,
         hott_dst_s,
         grow_s,
-        cols_s,
         weight_s,
-        pre_s,
-        pulled_s,
-        msg_s,
-        dpre_s,
-        keep,
-        swap_out,
-        swap_in,
-        x_out,
-        x_in,
+        sum_s,
         rows_out,
         rows_in,
         ga,
@@ -94,10 +87,8 @@
         b1,
         b2,
         load_sem,
-        full_send,
-        full_recv,
-        rs_send,
-        rs_recv,
+        in_send,
+        in_recv,
         row_send,
         row_recv,
         sum_send,
@@ -147,116 +138,127 @@
     for peer in graph_peers:
         pl.semaphore_signal(barrier, inc=1, device_id=peer, device_id_type=MESH)
 
-    places = (
-        atoms_ref,
-        cot_ref,
-        src_ref,
-        dst_ref,
-        left_s.at[:, pl.ds(0, NR)],
-        env_ref,
-        right_s.at[pl.ds(NR, DA)],
-        right_s.at[pl.ds(0, NR)],
-        ow_ref,
-    )
+    held = (atoms_ref, cot_ref, src_ref, dst_ref, basis.at[g], env_ref, sw_ref, rw_ref, ow_ref)
     loads = []
-    for i, place in enumerate(places):
-        held = inputs[i].at[0] if i == 4 else inputs[i]
-        loads.append(pltpu.make_async_copy(held, place, load_sem.at[i]))
+    for i, ref in enumerate(held):
+        source = inputs[i].at[0] if i == 4 else inputs[i]
+        loads.append(pltpu.make_async_copy(source, ref, load_sem.at[i]))
+    for i in (0, 1, 2, 3, 5, 4, 6, 7, 8):
         loads[i].start()
 
     loads[0].wait()
     loads[1].wait()
-    stacked = jnp.concatenate([atoms_ref[0], cot_ref[0]], axis=0)
-    full1[g] = stacked[:PAD]
-    full2[g] = stacked[PAD:]
-    pl.semaphore_wait(barrier, 21)
-    for peer in graph_peers:
-        send(full1.at[g], full1.at[g], full_send.at[0], full_recv.at[0, g], peer)
-    for peer in graph_peers:
-        send(full2.at[g], full2.at[g], full_send.at[1], full_recv.at[1, g], peer)
-
+    full[g] = jnp.concatenate([atoms_ref[0], cot_ref[0]], axis=0)
     for i in (2, 3, 5):
         loads[i].wait()
-    src_row = src_ref[...]
-    dst_row = dst_ref[...]
     slots = lax.broadcasted_iota(jnp.int32, (1, EDGES), 1)
     live = (slots < count_ref[0, 0]).astype(F32)
-    src_padded = src_row + (PAD - OWN) * by_owner(src_row)
-    table = jnp.concatenate(
-        [src_padded.astype(F32), dst_row.astype(F32), env_ref[...] * live, jnp.zeros((5, EDGES), F32)], axis=0
-    )
-    cols_s[...] = table.T
-    hot_src_s[...] = hot(lax.broadcasted_iota(jnp.int32, (EDGES, 8 * PAD), 1).astype(F32) == cols_s[:, 0:1])
-    hot_dst_s[...] = hot(lax.broadcasted_iota(jnp.int32, (EDGES, ATOMS), 1).astype(F32) == cols_s[:, 1:2])
-    weight_s[...] = jnp.broadcast_to(cols_s[:, 2:3], (EDGES, COLS))
-    atom_rows = lax.broadcasted_iota(jnp.int32, (ATOMS, EDGES), 0)
-    hott_src_s[...] = hot(atom_rows == src_row)
-    hott_dst_s[...] = hot(atom_rows == dst_row)
-    at1_r = lax.broadcasted_iota(jnp.int32, (ATOMS, 8 * PAD), 0)
-    at1_c = lax.broadcasted_iota(jnp.int32, (ATOMS, 8 * PAD), 1)
-    at1 = at1_r + (PAD - OWN) * by_owner(at1_r)
-    pick_atoms = hot(at1_c == at1)
-    inner = at1_r - OWN * by_owner(at1_r)
-    pick_cot1 = hot((at1_c == at1 + OWN) & (inner < PAD - OWN))
-    at2_r = lax.broadcasted_iota(jnp.int32, (ATOMS, 8 * REST), 0)
-    at2_c = lax.broadcasted_iota(jnp.int32, (ATOMS, 8 * REST), 1)
-    owner2 = by_owner(at2_r)
-    inner2 = at2_r - OWN * owner2
-    pick_cot2 = hot((at2_c == owner2 * REST + inner2 - (PAD - OWN)) & (inner2 >= PAD - OWN))
-    for i in (4, 6, 7, 8):
-        loads[i].wait()
-
-    for peer in graph_peers:
-        arrived(full1.at[peer[1]], full_recv.at[0, peer[1]])
-    both = full1[...].reshape(8 * PAD, DA)
-    left_s[:, NR:] = dot(hot_src_s[...], both).astype(BF16)
-    for peer in graph_peers:
-        arrived(full2.at[peer[1]], full_recv.at[1, peer[1]])
-    cot = (dot(pick_cot1, both) + dot(pick_cot2, full2[...].reshape(8 * REST, DA))).astype(BF16)
-    cot_s[...] = cot
-    back_s[...] = (dot_nt(cot, ow_ref[...]) * scale).astype(BF16)
-
-    def pass_x(dx):
-        arrived(swap_in.at[dx], rs_recv.at[0, dx])
-        x_out[dx] = (keep[dx] + swap_in[dx].astype(F32)).astype(BF16)
-        send(x_out.at[dx], x_in.at[dx], rs_send.at[1, dx], rs_recv.at[1, dx], x_peer[dx])
-
-    before = None
-    for dx in (2, 1, 3, 0):
-        cols = pl.ds(pl.multiple_of(x_at[dx] * 2 * COLS, 2 * COLS), 2 * COLS)
-        pre_s[...] = dot(left_s[...], right_s[:, cols])
-        pulled_s[...] = dot(hot_dst_s[...], back_s[:, cols])
-        for r in range(8):
-            rows = slice(r * 64, (r + 1) * 64)
-            pre = pre_s[rows, :]
-            weight = jnp.concatenate([weight_s[rows, :]] * 2, axis=1)
-            sigma = 0.5 * jnp.tanh(0.5 * pre) + 0.5
-            silu = pre * sigma
-            msg_s[rows, :] = (silu * weight).astype(BF16)
-            slope = sigma + silu * (1.0 - sigma)
-            dpre_s[rows, :] = (pulled_s[rows, :] * weight * slope).astype(BF16)
-        for j, (picks, terms) in enumerate(((hott_dst_s, msg_s), (hott_src_s, dpre_s))):
-            part = dot(picks[...], terms[...])
-            low, high = part[:, :COLS], part[:, COLS:]
-            keep[dx, j] = jnp.where(core == 0, low, high)
-            swap_out[dx, j] = jnp.where(core == 0, high, low).astype(BF16)
-        send(swap_out.at[dx], swap_in.at[dx], rs_send.at[0, dx], rs_recv.at[0, dx], sibling)
-        if before:
-            pass_x(before)
-        before = dx
-
-    atoms_s[...] = dot(pick_atoms, both).astype(BF16)
-    atoms_t[...] = atoms_s[...].astype(F32).T.astype(BF16)
+    lines = (src_ref[...].astype(F32), dst_ref[...].astype(F32), env_ref[...] * live, jnp.zeros((1, EDGES), F32))
+    table[g] = jnp.concatenate([line[:, j * 128 : (j + 1) * 128] for line in lines for j in range(4)], axis=0)
+    loads[4].wait()
+    pl.semaphore_wait(barrier, 21)
+    gathered = (full, table, basis)
+
+    def offer(n, k):
+        buf = gathered[n]
+        send(buf.at[g], buf.at[g], in_send.at[n, k], in_recv.at[n, g], x_peer[k] if k else sibling)
+
+    for n in range(3):
+        for k in (2, 1, 3, 0):
+            if n < 2 or k != 2:
+                offer(n, k)
+
+    def block(k, c):
+        return 2 * x_at[k] + c
+
+    def relay(n, k):
+        b = block(k, core)
+        buf = gathered[n]
+        arrived(buf.at[b], in_recv.at[n, b])
+        send(buf.at[b], buf.at[b], in_send.at[n, 3 + k], in_recv.at[n, b], sibling)
+
+    def select(b):
+        lines = table[b]
+        columns = lines.T
+        row_atom = lax.broadcasted_iota(jnp.int32, (ATOMS, 128), 0).astype(F32)
+        col_atom = lax.broadcasted_iota(jnp.int32, (128, ATOMS), 1).astype(F32)
+        for j in range(4):
+            edges = pl.ds(j * 128, 128)
+            hot_src_s[b, edges, :] = hot(col_atom == columns[:, j : j + 1])
+            hot_dst_s[b, edges, :] = hot(col_atom == columns[:, 4 + j : 5 + j])
+            weight_s[b, edges, :] = jnp.broadcast_to(columns[:, 8 + j : 9 + j], (128, COLS))
+            hott_src_s[b, :, edges] = hot(row_atom == lines[j : j + 1, :])
+            hott_dst_s[b, :, edges] = hot(row_atom == lines[4 + j : 5 + j, :])
+
+    select(g)
+    pick_r = lax.broadcasted_iota(jnp.int32, (ATOMS, 8 * SLOT), 0)
+    pick_c = lax.broadcasted_iota(jnp.int32, (ATOMS, 8 * SLOT), 1)
+    pick_at = pick_r + OWN * by_owner(pick_r)
+    pick_atoms = hot(pick_c == pick_at)
+    pick_cot = hot(pick_c == pick_at + OWN)
     grow_r = lax.broadcasted_iota(jnp.int32, (8 * PAD, ATOMS), 0)
     grow_c = lax.broadcasted_iota(jnp.int32, (8 * PAD, ATOMS), 1)
     inner = grow_r & (PAD - 1)
     grow_s[...] = hot((inner < OWN) & (grow_c == (grow_r >> 5) * OWN + inner))
-    arrived(swap_in.at[0], rs_recv.at[0, 0])
-    total = keep[0] + swap_in[0].astype(F32)
-    for dx in (2, 1, 3):
-        arrived(x_in.at[dx], rs_recv.at[1, dx])
-        total = total + x_in[dx].astype(F32)
-    sums = total.astype(BF16)
+    for i in (6, 7, 8):
+        loads[i].wait()
+    for k in (1, 3, 2):
+        relay(0, k)
+    offer(2, 2)
+    for k in (1, 3, 2):
+        relay(1, k)
+    for k in range(4):
+        arrived(full.at[block(k, other)], in_recv.at[0, block(k, other)])
+    both = full[...].reshape(8 * SLOT, DA)
+    atoms = dot(pick_atoms, both).astype(BF16)
+    cot = dot(pick_cot, both).astype(BF16)
+    atoms_s[...] = atoms
+    cot_s[...] = cot
+    own_cols = pl.ds(pl.multiple_of(g * COLS, COLS), COLS)
+    product = dot(atoms, sw_ref[:, own_cols])
+    high = product.astype(BF16)
+    rows_s[:, :COLS] = high
+    rows_s[:, COLS:] = (product - high.astype(F32)).astype(BF16)
+    back_s[...] = (dot_nt(cot, ow_ref[own_cols, :]) * scale).astype(BF16)
+
+    def edges_of(b):
+        at_src = dot(hot_src_s[b], rows_s[...])
+        pre = dot(basis[b], rw_ref[:, own_cols]) + at_src[:, :COLS] + at_src[:, COLS:]
+        pulled = dot(hot_dst_s[b], back_s[...])
+        weight = weight_s[b]
+        sigma = 0.5 * jnp.tanh(0.5 * pre) + 0.5
+        silu = pre * sigma
+        slope = sigma + silu * (1.0 - sigma)
+        message = (silu * weight).astype(BF16)
+        dpre = (pulled * weight * slope).astype(BF16)
+        return dot(hott_dst_s[b], message), dot(hott_src_s[b], dpre)
+
+    def add(b):
+        first, second = edges_of(b)
+        sum_s[0] += first
+        sum_s[1] += second
+
+    sum_s[0], sum_s[1] = edges_of(g)
+    atoms_t[...] = atoms_s[...].astype(F32).T.astype(BF16)
+    for k in (0, 1, 3, 2):
+        if k:
+            select(block(k, core))
+        arrived(table.at[block(k, other)], in_recv.at[1, block(k, other)])
+        select(block(k, other))
+    arrived(basis.at[block(0, other)], in_recv.at[2, block(0, other)])
+    add(block(0, other))
+    for k in (1, 3):
+        relay(2, k)
+    add(block(1, core))
+    add(block(3, core))
+    for k in (1, 3):
+        arrived(basis.at[block(k, other)], in_recv.at[2, block(k, other)])
+        add(block(k, other))
+    relay(2, 2)
+    add(block(2, core))
+    arrived(basis.at[block(2, other)], in_recv.at[2, block(2, other)])
+    add(block(2, other))
+    sums = sum_s[...].astype(BF16)
     summed, dsum = sums[0], sums[1]
 
     ga[...] = dot_tn(summed, cot_s[...]).astype(BF16).reshape(SIDE, 16, DA)
@@ -267,7 +269,6 @@
 
     rows_out[:, 0] = dot(grow_s[...], summed).astype(BF16).reshape(8, PAD, COLS)
     rows_out[:, 1] = dot(grow_s[...], dsum).astype(BF16).reshape(8, PAD, COLS)
-    own_cols = pl.ds(pl.multiple_of(g * COLS, COLS), COLS)
     rows_in[:, :, own_cols] = rows_out[g]
     for peer in graph_peers:
         send(rows_out.at[peer[1]], rows_in.at[:, :, own_cols], row_send, row_recv.at[g], peer)
@@ -291,7 +292,7 @@
         arrived(rows_in.at[:, :, peer_cols], row_recv.at[peer[1]])
     update = dot(rows_in[0], ow_ref[...]) * scale
     updated_ref[0] = (atoms_ref[0].astype(F32) + update[:OWN]).astype(BF16)
-    pushed = dot_nt(rows_in[1], right_s[NR:, :])
+    pushed = dot_nt(rows_in[1], sw_ref[...])
     grad_atoms_ref[0] = (cot_ref[0].astype(F32) + pushed[:OWN]).astype(BF16)
 
     arrived(pa.at[pl.ds(1, 7)], sum_recv.at[2])
@@ -410,12 +411,9 @@
         sent(buf.at[core, 0, pl.ds(1, 7 if n < 2 else 3)], g_send.at[n, 0])
         sent(buf.at[core, pl.ds(1, 3 if n < 2 else 7)], g_send.at[n, 1])
         sent(buf.at[core], g_send.at[n, 2])
-    sent(full1.at[pl.ds(0, 7)], full_send.at[0])
-    sent(full2.at[pl.ds(0, 7)], full_send.at[1])
-    for dx in range(4):
-        sent(swap_out.at[dx], rs_send.at[0, dx])
-        if dx:
-            sent(x_out.at[dx], rs_send.at[1, dx])
+    for n, buf in enumerate(gathered):
+        for k in range(7):
+            sent(buf.at[0], in_send.at[n, k])
     sent(rows_out.at[pl.ds(0, 7)], row_send)
     sent(ra.at[pl.ds(1, 7)], sum_send.at[0])
     sent(rb.at[pl.ds(1, 7)], sum_send.at[1])
@@ -435,8 +433,8 @@
 def local(atoms, cotangent, sources, targets, radial, envelope, edge_counts, source_weight, radial_weight, output_weight):
     inputs = (atoms, cotangent, sources, targets, radial, envelope, source_weight, radial_weight, output_weight)
     vmem = pl.BlockSpec(memory_space=pltpu.VMEM)
+    hbm = pl.BlockSpec(memory_space=pltpu.HBM)
     smem = pl.BlockSpec(memory_space=pltpu.SMEM)
-    hbm = pl.BlockSpec(memory_space=pltpu.HBM)
     dma = pltpu.SemaphoreType.DMA
 
     def like(a):
@@ -459,30 +457,23 @@
             like(targets),
             like(envelope),
             like(output_weight),
-            pltpu.VMEM((EDGES, NR + DA), BF16),
-            pltpu.VMEM((NR + DA, DE), BF16),
-            pltpu.VMEM((8, PAD, DA), BF16),
-            pltpu.VMEM((8, REST, DA), BF16),
+            like(radial_weight),
+            like(source_weight),
+            pltpu.VMEM((8, EDGES, NR), BF16),
+            pltpu.VMEM((8, 16, 128), F32),
+            pltpu.VMEM((8, SLOT, DA), BF16),
             pltpu.VMEM((ATOMS, DA), BF16),
             pltpu.VMEM((DA, ATOMS), BF16),
             pltpu.VMEM((ATOMS, DA), BF16),
-            pltpu.VMEM((ATOMS, DE), BF16),
-            pltpu.VMEM((EDGES, 8 * PAD), BF16),
-            pltpu.VMEM((EDGES, ATOMS), BF16),
-            pltpu.VMEM((ATOMS, EDGES), BF16),
-            pltpu.VMEM((ATOMS, EDGES), BF16),
+            pltpu.VMEM((ATOMS, 2 * COLS), BF16),
+            pltpu.VMEM((ATOMS, COLS), BF16),
+            pltpu.VMEM((8, EDGES, ATOMS), BF16),
+            pltpu.VMEM((8, EDGES, ATOMS), BF16),
+            pltpu.VMEM((8, ATOMS, EDGES), BF16),
+            pltpu.VMEM((8, ATOMS, EDGES), BF16),
             pltpu.VMEM((8 * PAD, ATOMS), BF16),
-            pltpu.VMEM((EDGES, 8), F32),
-            pltpu.VMEM((EDGES, COLS), F32),
-            pltpu.VMEM((EDGES, 2 * COLS), F32),
-            pltpu.VMEM((EDGES, 2 * COLS), F32),
-            pltpu.VMEM((EDGES, 2 * COLS), BF16),
-            pltpu.VMEM((EDGES, 2 * COLS), BF16),
-            pltpu.VMEM((4, 2, ATOMS, COLS), F32),
-            pltpu.VMEM((4, 2, ATOMS, COLS), BF16),
-            pltpu.VMEM((4, 2, ATOMS, COLS), BF16),
-            pltpu.VMEM((4, 2, ATOMS, COLS), BF16),
-            pltpu.VMEM((4, 2, ATOMS, COLS), BF16),
+            pltpu.VMEM((8, EDGES, COLS), F32),
+            pltpu.VMEM((2, ATOMS, COLS), F32),
             pltpu.VMEM((8, 2, PAD, COLS), BF16),
             pltpu.VMEM((2, PAD, DE), BF16),
             pltpu.VMEM((SIDE, 16, DA), BF16),
@@ -496,10 +487,8 @@
             pltpu.VMEM((2, 4, SIDE, 32, COLS), BF16),
             pltpu.VMEM((2, SIDE, 4, 32, COLS), BF16),
             dma((9,)),
-            dma((2,)),
-            dma((2, 8)),
-            dma((2, 4)),
-            dma((2, 4)),
+            dma((3, 7)),
+            dma((3, 8)),
             dma,
             dma((8,)),
             dma((4,)),

time: 58.3 us -> 56.7 us (0.973)
  Pallas kernels: 56.9 us -> 55.2 us
    pallas_call x1, Pallas kernels: 55.5 us -> 53.9 us  [local(): pl.pallas_call(body, out_shape=(pltpu.VMEM((1, OWN, DA), BF16), pltpu.VME...]
where the time goes in v4:
time: 56.7 us; the launch traced here: 56.5 us
  Pallas kernels  55.2 us (97%)
  between operations  1.29 us (2%)
    pallas_call x1, Pallas kernels, local(): pl.pallas_call(body, out_shape=(pltpu.VMEM((1, OWN, DA), BF16), pltpu.VME...  53.9 us
    pallas_call x1, Pallas kernels, local(): pl.pallas_call(place, out_shape=tuple((jax.ShapeDtypeStruct(a.shape, a.dt...  1.37 us

profile of v4, /device:TPU:1, one launch (start us, length us, event | category | flops | bytes accessed | tf_op | source)
XLA Modules:
  0.0 56.5 jit_solution(4423889960390938663)
XLA Ops:
  1.3 53.9 %shard_map.129 = (bf16[1,24,512]{2,1,0:T(8,128)(2,1)S(1)}, bf16[1,24,512]{2,1,0:T(8,128)(2,1)S(1)}, bf16[8,8,16,512]{3,2,1,0:T(8,128)(2,1)S(1)}, bf16[512,1024]{1,0:T(8,128)(2,1)S(1)}) custom-call(s32[1,1]{1,0:T(1,128)S(6)} %copy.14.count_ref, bf16[1,24,512]{2,1,0:T(8,128)(2,1)} %refs_0_.1, bf16[1,24,512]{2,1,0:T(8,128)(2,1)} %refs_1_.1, s32[1,512]{1,0:T(1,128)} %refs_2_.1, ...), custom_call_target="tpu_custom_call" | custom-call | tf_op jit(solution)/shard_map/pallas_call | solution.py:443
  55.1 1.4 %shard_map.130 = (bf16[1,24,512]{2,1,0:T(8,128)(2,1)}, bf16[1,24,512]{2,1,0:T(8,128)(2,1)}, bf16[512,1024]{1,0:T(8,128)(2,1)}, bf16[1024,512]{1,0:T(8,128)(2,1)}) custom-call(bf16[1,24,512]{2,1,0:T(8,128)(2,1)S(1)} %get-tuple-element.8.refs_0_, bf16[1,24,512]{2,1,0:T(8,128)(2,1)S(1)} %get-tuple-element.9.refs_1_, ...), custom_call_target="tpu_custom_call" | custom-call | tf_op jit(solution)/shard_map/pallas_call | solution.py:506

commit v5 on v4

--- a/solution.py
+++ b/solution.py
@@ -132,12 +132,8 @@
     graph_peers = [x_peer[2], x_peer_other[2], x_peer[1], x_peer_other[1], x_peer[3], x_peer_other[3], sibling]
 
     barrier = pltpu.get_barrier_semaphore()
-    for k in reversed(NEAR[1:]):
-        for peer in (y_peer[k], z_peer[k]):
-            pl.semaphore_signal(barrier, inc=1, device_id=peer, device_id_type=MESH)
     for peer in graph_peers:
         pl.semaphore_signal(barrier, inc=1, device_id=peer, device_id_type=MESH)
-
     held = (atoms_ref, cot_ref, src_ref, dst_ref, basis.at[g], env_ref, sw_ref, rw_ref, ow_ref)
     loads = []
     for i, ref in enumerate(held):
@@ -145,6 +141,9 @@
         loads.append(pltpu.make_async_copy(source, ref, load_sem.at[i]))
     for i in (0, 1, 2, 3, 5, 4, 6, 7, 8):
         loads[i].start()
+    for k in reversed(NEAR[1:]):
+        for peer in (y_peer[k], z_peer[k]):
+            pl.semaphore_signal(barrier, inc=1, device_id=peer, device_id_type=MESH)
 
     loads[0].wait()
     loads[1].wait()
@@ -163,7 +162,7 @@
         buf = gathered[n]
         send(buf.at[g], buf.at[g], in_send.at[n, k], in_recv.at[n, g], x_peer[k] if k else sibling)
 
-    for n in range(3):
+    for n in (1, 0, 2):
         for k in (2, 1, 3, 0):
             if n < 2 or k != 2:
                 offer(n, k)
@@ -200,13 +199,19 @@
     grow_c = lax.broadcasted_iota(jnp.int32, (8 * PAD, ATOMS), 1)
     inner = grow_r & (PAD - 1)
     grow_s[...] = hot((inner < OWN) & (grow_c == (grow_r >> 5) * OWN + inner))
-    for i in (6, 7, 8):
-        loads[i].wait()
-    for k in (1, 3, 2):
-        relay(0, k)
+    arrived(table.at[block(0, other)], in_recv.at[1, block(0, other)])
+    select(block(0, other))
     offer(2, 2)
     for k in (1, 3, 2):
         relay(1, k)
+    for k in (1, 3, 2):
+        select(block(k, core))
+        relay(0, k)
+    for k in (1, 3, 2):
+        arrived(table.at[block(k, other)], in_recv.at[1, block(k, other)])
+        select(block(k, other))
+    for i in (6, 7, 8):
+        loads[i].wait()
     for k in range(4):
         arrived(full.at[block(k, other)], in_recv.at[0, block(k, other)])
     both = full[...].reshape(8 * SLOT, DA)
@@ -239,18 +244,13 @@
         sum_s[1] += second
 
     sum_s[0], sum_s[1] = edges_of(g)
-    atoms_t[...] = atoms_s[...].astype(F32).T.astype(BF16)
-    for k in (0, 1, 3, 2):
-        if k:
-            select(block(k, core))
-        arrived(table.at[block(k, other)], in_recv.at[1, block(k, other)])
-        select(block(k, other))
     arrived(basis.at[block(0, other)], in_recv.at[2, block(0, other)])
     add(block(0, other))
     for k in (1, 3):
         relay(2, k)
     add(block(1, core))
     add(block(3, core))
+    atoms_t[...] = atoms_s[...].astype(F32).T.astype(BF16)
     for k in (1, 3):
         arrived(basis.at[block(k, other)], in_recv.at[2, block(k, other)])
         add(block(k, other))
@@ -423,7 +423,12 @@
 
 def place(*refs):
     sems = refs[8]
-    copies = [pltpu.make_async_copy(refs[i], refs[4 + i], sems.at[i]) for i in range(4)]
+    copies = [pltpu.make_async_copy(refs[i], refs[4 + i], sems.at[i]) for i in range(2)]
+    for i in (2, 3):
+        rows = refs[i].shape[0] // 8
+        for j in range(8):
+            part = pl.ds(j * rows, rows)
+            copies.append(pltpu.make_async_copy(refs[i].at[part], refs[4 + i].at[part], sems.at[len(copies)]))
     for c in copies:
         c.start()
     for c in copies:
@@ -508,7 +513,7 @@
         out_shape=tuple(jax.ShapeDtypeStruct(a.shape, a.dtype) for a in results),
         in_specs=[vmem] * 4,
         out_specs=(hbm,) * 4,
-        scratch_shapes=[dma((4,))],
+        scratch_shapes=[dma((18,))],
     )(*(pltpu.with_memory_space_constraint(a, pltpu.VMEM) for a in results))
 
 

time: 56.7 us -> 55.7 us (0.982)
  Pallas kernels: 55.2 us -> 54.3 us
    pallas_call x1, Pallas kernels: 53.9 us -> 52.8 us  [local(): pl.pallas_call(body, out_shape=(pltpu.VMEM((1, OWN, DA), BF16), pltpu.VME...]
where the time goes in v5:
time: 55.7 us; the launch traced here: 55.6 us
  Pallas kernels  54.3 us (97%)
  between operations  1.29 us (2%)
    pallas_call x1, Pallas kernels, local(): pl.pallas_call(body, out_shape=(pltpu.VMEM((1, OWN, DA), BF16), pltpu.VME...  52.8 us
    pallas_call x1, Pallas kernels, local(): pl.pallas_call(place, out_shape=tuple((jax.ShapeDtypeStruct(a.shape, a.dt...  1.47 us

profile of v5, /device:TPU:1, one launch (start us, length us, event | category | flops | bytes accessed | tf_op | source)
XLA Modules:
  0.0 55.6 jit_solution(2065469152700071598)
XLA Ops:
  1.3 52.8 %shard_map.129 = (bf16[1,24,512]{2,1,0:T(8,128)(2,1)S(1)}, bf16[1,24,512]{2,1,0:T(8,128)(2,1)S(1)}, bf16[8,8,16,512]{3,2,1,0:T(8,128)(2,1)S(1)}, bf16[512,1024]{1,0:T(8,128)(2,1)S(1)}) custom-call(s32[1,1]{1,0:T(1,128)S(6)} %copy.14.count_ref, bf16[1,24,512]{2,1,0:T(8,128)(2,1)} %refs_0_.1, bf16[1,24,512]{2,1,0:T(8,128)(2,1)} %refs_1_.1, s32[1,512]{1,0:T(1,128)} %refs_2_.1, ...), custom_call_target="tpu_custom_call" | custom-call | tf_op jit(solution)/shard_map/pallas_call | solution.py:448
  54.1 1.5 %shard_map.130 = (bf16[1,24,512]{2,1,0:T(8,128)(2,1)}, bf16[1,24,512]{2,1,0:T(8,128)(2,1)}, bf16[512,1024]{1,0:T(8,128)(2,1)}, bf16[1024,512]{1,0:T(8,128)(2,1)}) custom-call(bf16[1,24,512]{2,1,0:T(8,128)(2,1)S(1)} %get-tuple-element.8.refs_0_, bf16[1,24,512]{2,1,0:T(8,128)(2,1)S(1)} %get-tuple-element.9.refs_1_, ...), custom_call_target="tpu_custom_call" | custom-call | tf_op jit(solution)/shard_map/pallas_call | solution.py:511

commit v6 on v5

--- a/solution.py
+++ b/solution.py
@@ -238,33 +238,32 @@
         dpre = (pulled * weight * slope).astype(BF16)
         return dot(hott_dst_s[b], message), dot(hott_src_s[b], dpre)
 
-    def add(b):
-        first, second = edges_of(b)
-        sum_s[0] += first
-        sum_s[1] += second
-
-    sum_s[0], sum_s[1] = edges_of(g)
+    def add(*blocks):
+        terms = [edges_of(b) for b in blocks]
+        for i in range(2):
+            sum_s[i] += sum((term[i] for term in terms[1:]), terms[0][i])
+
+    sum_s[...] = jnp.zeros_like(sum_s)
     arrived(basis.at[block(0, other)], in_recv.at[2, block(0, other)])
-    add(block(0, other))
+    add(g, block(0, other))
     for k in (1, 3):
         relay(2, k)
-    add(block(1, core))
-    add(block(3, core))
+    add(block(1, core), block(3, core))
     atoms_t[...] = atoms_s[...].astype(F32).T.astype(BF16)
     for k in (1, 3):
         arrived(basis.at[block(k, other)], in_recv.at[2, block(k, other)])
-        add(block(k, other))
     relay(2, 2)
-    add(block(2, core))
+    add(block(1, other), block(3, other), block(2, core))
     arrived(basis.at[block(2, other)], in_recv.at[2, block(2, other)])
     add(block(2, other))
     sums = sum_s[...].astype(BF16)
     summed, dsum = sums[0], sums[1]
 
-    ga[...] = dot_tn(summed, cot_s[...]).astype(BF16).reshape(SIDE, 16, DA)
+    ga[...] = dot(sum_s[0].T.astype(BF16), cot_s[...]).astype(BF16).reshape(SIDE, 16, DA)
+    for k in reversed(NEAR[1:]):
+        send(ga.at[y_at[k]], ra.at[k], sum_send.at[0], sum_recv.at[0], y_peer[k])
     gb[...] = dot(atoms_t[...], dsum).astype(BF16).reshape(SIDE, 64, COLS)
     for k in reversed(NEAR[1:]):
-        send(ga.at[y_at[k]], ra.at[k], sum_send.at[0], sum_recv.at[0], y_peer[k])
         send(gb.at[z_at[k]], rb.at[k], sum_send.at[1], sum_recv.at[1], z_peer[k])
 
     rows_out[:, 0] = dot(grow_s[...], summed).astype(BF16).reshape(8, PAD, COLS)
@@ -273,18 +272,19 @@
     for peer in graph_peers:
         send(rows_out.at[peer[1]], rows_in.at[:, :, own_cols], row_send, row_recv.at[g], peer)
 
+    def total(own, parts):
+        acc = own.astype(F32)
+        for k in range(1, SIDE):
+            acc = acc + parts[k].astype(F32)
+        return acc.astype(BF16)
+
     arrived(ra.at[pl.ds(1, 7)], sum_recv.at[0])
-    arrived(rb.at[pl.ds(1, 7)], sum_recv.at[1])
-    sum_a = ga[y].astype(F32)
-    sum_b = gb[z].astype(F32)
-    for k in range(1, SIDE):
-        sum_a = sum_a + ra[k].astype(F32)
-        sum_b = sum_b + rb[k].astype(F32)
-
-    pa[0] = sum_a.astype(BF16)
-    pb[0] = sum_b.astype(BF16)
+    pa[0] = total(ga[y], ra)
     for k in reversed(NEAR[1:]):
         send(pa.at[0], pa.at[k], sum_send.at[2], sum_recv.at[2], z_peer[k])
+    arrived(rb.at[pl.ds(1, 7)], sum_recv.at[1])
+    pb[0] = total(gb[z], rb)
+    for k in reversed(NEAR[1:]):
         send(pb.at[0], pb.at[k], sum_send.at[3], sum_recv.at[3], y_peer[k])
 
     for peer in graph_peers:
@@ -295,20 +295,13 @@
     pushed = dot_nt(rows_in[1], sw_ref[...])
     grad_atoms_ref[0] = (cot_ref[0].astype(F32) + pushed[:OWN]).astype(BF16)
 
-    arrived(pa.at[pl.ds(1, 7)], sum_recv.at[2])
-    arrived(pb.at[pl.ds(1, 7)], sum_recv.at[3])
-    sum_a = pa[z].astype(F32)
-    sum_b = pb[y].astype(F32)
-    for j in range(1, SIDE):
-        sum_a = sum_a + pa[lax.rem(z + SIDE - j, SIDE)].astype(F32)
-        sum_b = sum_b + pb[lax.rem(y + SIDE - j, SIDE)].astype(F32)
+    def settle(at, parts, factor):
+        acc = parts[at].astype(F32)
+        for j in range(1, SIDE):
+            acc = acc + parts[lax.rem(at + SIDE - j, SIDE)].astype(F32)
+        return (acc * factor).astype(BF16)
+
     systems = SIDE * SIDE
-    piece_a = (sum_a * (scale / math.sqrt(systems * ATOMS))).astype(BF16)
-    piece_b = (sum_b * (16.0 / math.sqrt(systems * 8 * EDGES))).astype(BF16)
-    a1[core, 0, 0] = piece_a[:, : DA // 2]
-    a2[core, 0, 0] = piece_a[:, DA // 2 :]
-    b1[core, 0, 0] = piece_b[:32]
-    b2[core, 0, 0] = piece_b[32:]
 
     back_to = [[y_peer[(SIDE - k) % SIDE] for k in NEAR], [z_peer[(SIDE - k) % SIDE] for k in NEAR]]
     back_x = [x_peer[(4 - k) % 4] for k in NEAR_X]
@@ -347,10 +340,21 @@
             sibling,
         )
 
-    for buf, n, peers in second:
+    for turn in range(2):
+        if turn == 0:
+            arrived(pa.at[pl.ds(1, 7)], sum_recv.at[2])
+            piece = settle(z, pa, scale / math.sqrt(systems * ATOMS))
+            a1[core, 0, 0] = piece[:, : DA // 2]
+            a2[core, 0, 0] = piece[:, DA // 2 :]
+        else:
+            arrived(pb.at[pl.ds(1, 7)], sum_recv.at[3])
+            piece = settle(y, pb, 16.0 / math.sqrt(systems * 8 * EDGES))
+            b1[core, 0, 0] = piece[:32]
+            b2[core, 0, 0] = piece[32:]
+        buf, n, peers = second[turn]
         for s in (3, 1, 2):
             send(buf.at[core, 0, 0], buf.at[core, 0, s], g_send.at[n, 0], near_recv.at[n, 0 if s < 3 else 1], back_x[s])
-    for buf, n, peers in first:
+        buf, n, peers = first[turn]
         for s in range(7, 0, -1):
             send(buf.at[core, 0, 0], buf.at[core, 0, s], g_send.at[n, 0], near_recv.at[n, group_of(s)], peers[s])
         pass_first(buf, n, 0, 1)

time: 55.7 us -> 54.6 us (0.980)
  Pallas kernels: 54.3 us -> 53.1 us
    pallas_call x1, Pallas kernels: 52.8 us -> 51.7 us  [local(): pl.pallas_call(body, out_shape=(pltpu.VMEM((1, OWN, DA), BF16), pltpu.VME...]
where the time goes in v6:
time: 54.6 us; the launch traced here: 54.4 us
  Pallas kernels  53.1 us (97%)
  between operations  1.29 us (2%)
    pallas_call x1, Pallas kernels, local(): pl.pallas_call(body, out_shape=(pltpu.VMEM((1, OWN, DA), BF16), pltpu.VME...  51.7 us
    pallas_call x1, Pallas kernels, local(): pl.pallas_call(place, out_shape=tuple((jax.ShapeDtypeStruct(a.shape, a.dt...  1.47 us

profile of v6, /device:TPU:1, one launch (start us, length us, event | category | flops | bytes accessed | tf_op | source)
XLA Modules:
  0.0 54.4 jit_solution(3101129743408840456)
XLA Ops:
  1.3 51.7 %shard_map.129 = (bf16[1,24,512]{2,1,0:T(8,128)(2,1)S(1)}, bf16[1,24,512]{2,1,0:T(8,128)(2,1)S(1)}, bf16[8,8,16,512]{3,2,1,0:T(8,128)(2,1)S(1)}, bf16[512,1024]{1,0:T(8,128)(2,1)S(1)}) custom-call(s32[1,1]{1,0:T(1,128)S(6)} %copy.14.count_ref, bf16[1,24,512]{2,1,0:T(8,128)(2,1)} %refs_0_.1, bf16[1,24,512]{2,1,0:T(8,128)(2,1)} %refs_1_.1, s32[1,512]{1,0:T(1,128)} %refs_2_.1, ...), custom_call_target="tpu_custom_call" | custom-call | tf_op jit(solution)/shard_map/pallas_call | solution.py:452
  53.0 1.5 %shard_map.130 = (bf16[1,24,512]{2,1,0:T(8,128)(2,1)}, bf16[1,24,512]{2,1,0:T(8,128)(2,1)}, bf16[512,1024]{1,0:T(8,128)(2,1)}, bf16[1024,512]{1,0:T(8,128)(2,1)}) custom-call(bf16[1,24,512]{2,1,0:T(8,128)(2,1)S(1)} %get-tuple-element.8.refs_0_, bf16[1,24,512]{2,1,0:T(8,128)(2,1)S(1)} %get-tuple-element.9.refs_1_, ...), custom_call_target="tpu_custom_call" | custom-call | tf_op jit(solution)/shard_map/pallas_call | solution.py:515

commit v7 on v6

--- a/solution.py
+++ b/solution.py
@@ -238,14 +238,17 @@
         dpre = (pulled * weight * slope).astype(BF16)
         return dot(hott_dst_s[b], message), dot(hott_src_s[b], dpre)
 
+    def terms_of(*blocks):
+        terms = [edges_of(b) for b in blocks]
+        return [sum((term[i] for term in terms[1:]), terms[0][i]) for i in range(2)]
+
     def add(*blocks):
-        terms = [edges_of(b) for b in blocks]
+        terms = terms_of(*blocks)
         for i in range(2):
-            sum_s[i] += sum((term[i] for term in terms[1:]), terms[0][i])
-
-    sum_s[...] = jnp.zeros_like(sum_s)
+            sum_s[i] += terms[i]
+
     arrived(basis.at[block(0, other)], in_recv.at[2, block(0, other)])
-    add(g, block(0, other))
+    sum_s[0], sum_s[1] = terms_of(g, block(0, other))
     for k in (1, 3):
         relay(2, k)
     add(block(1, core), block(3, core))
@@ -255,11 +258,11 @@
     relay(2, 2)
     add(block(1, other), block(3, other), block(2, core))
     arrived(basis.at[block(2, other)], in_recv.at[2, block(2, other)])
-    add(block(2, other))
-    sums = sum_s[...].astype(BF16)
-    summed, dsum = sums[0], sums[1]
-
-    ga[...] = dot(sum_s[0].T.astype(BF16), cot_s[...]).astype(BF16).reshape(SIDE, 16, DA)
+    last = terms_of(block(2, other))
+    first_sum = sum_s[0] + last[0]
+    summed, dsum = first_sum.astype(BF16), (sum_s[1] + last[1]).astype(BF16)
+
+    ga[...] = dot(first_sum.T.astype(BF16), cot_s[...]).astype(BF16).reshape(SIDE, 16, DA)
     for k in reversed(NEAR[1:]):
         send(ga.at[y_at[k]], ra.at[k], sum_send.at[0], sum_recv.at[0], y_peer[k])
     gb[...] = dot(atoms_t[...], dsum).astype(BF16).reshape(SIDE, 64, COLS)

time: 54.6 us -> 54.6 us (level)
  no operation moved by 1% of the time
where the time goes in v7:
time: 54.6 us; the launch traced here: 54.4 us
  Pallas kernels  53.1 us (97%)
  between operations  1.29 us (2%)
    pallas_call x1, Pallas kernels, local(): pl.pallas_call(body, out_shape=(pltpu.VMEM((1, OWN, DA), BF16), pltpu.VME...  51.7 us
    pallas_call x1, Pallas kernels, local(): pl.pallas_call(place, out_shape=tuple((jax.ShapeDtypeStruct(a.shape, a.dt...  1.47 us

profile of v7, /device:TPU:1, one launch (start us, length us, event | category | flops | bytes accessed | tf_op | source)
XLA Modules:
  0.0 54.4 jit_solution(3101129743408840456)
XLA Ops:
  1.3 51.7 %shard_map.129 = (bf16[1,24,512]{2,1,0:T(8,128)(2,1)S(1)}, bf16[1,24,512]{2,1,0:T(8,128)(2,1)S(1)}, bf16[8,8,16,512]{3,2,1,0:T(8,128)(2,1)S(1)}, bf16[512,1024]{1,0:T(8,128)(2,1)S(1)}) custom-call(s32[1,1]{1,0:T(1,128)S(6)} %copy.14.count_ref, bf16[1,24,512]{2,1,0:T(8,128)(2,1)} %refs_0_.1, bf16[1,24,512]{2,1,0:T(8,128)(2,1)} %refs_1_.1, s32[1,512]{1,0:T(1,128)} %refs_2_.1, ...), custom_call_target="tpu_custom_call" | custom-call | tf_op jit(solution)/shard_map/pallas_call | solution.py:455
  53.0 1.5 %shard_map.130 = (bf16[1,24,512]{2,1,0:T(8,128)(2,1)}, bf16[1,24,512]{2,1,0:T(8,128)(2,1)}, bf16[512,1024]{1,0:T(8,128)(2,1)}, bf16[1024,512]{1,0:T(8,128)(2,1)}) custom-call(bf16[1,24,512]{2,1,0:T(8,128)(2,1)S(1)} %get-tuple-element.8.refs_0_, bf16[1,24,512]{2,1,0:T(8,128)(2,1)S(1)} %get-tuple-element.9.refs_1_, ...), custom_call_target="tpu_custom_call" | custom-call | tf_op jit(solution)/shard_map/pallas_call | solution.py:518
